TPU v7x, 256 devices: a whole 4x4x8 slice. The times are simulated.
256 devices in a mesh: occ: 16 (over x, z_hi, core), vir: 16 (over y, z_lo).
Axes of the slice: x: 4, y: 4, z: 8 (z_hi: 2, z_lo: 4; z = z_hi * 4 + z_lo), core: 2. Of those that a mesh axis runs over, the one named last changes fastest.
Arguments:
- amplitudes: bfloat16 [16384, 2048], P('occ', 'vir'), may hold values from -6 to 6
- integrals: bfloat16 [2048, 32768], P('occ', 'vir'), may hold values from -0.25 to 0.25
- contract_class: int32 [16], replicated, may hold values from 0 to 7, as said below
- column_class: int32 [256], P('vir'), may hold values from 0 to 7, as said below
Outputs:
- residual: float32 [16384, 32768], P('occ', 'vir')
Inputs may be any that keep to these rules, and one draw needn't show every extreme that they name: `contract_class`: each class 0 to 7 labels exactly 2 of the contracted pair tiles. `column_class`: every class 0 to 7 occurs among the tiles; the 16 tiles of one index of vir may all share one class.
All inputs are finite; a program needn't handle non-finite values.
Results may differ from a plain program's by a relative error of at most 0.0003.
Values may be sent and summed in bfloat16 or wider, within the bound.
No kernel may reach another device: no remote copies, remote signals or barrier semaphores. Data moves between devices by JAX's collectives and lax.ppermute only.
A program may use at most 128 MiB of HBM per device.

v0:
```python
import jax
import jax.numpy as jnp
from jax import lax
from jax.sharding import PartitionSpec as P

P_SIZE = 128


def accumulate(amp_piece, int_piece, contract_class, column_class):
    count = amp_piece.shape[1]
    tiles = count // P_SIZE
    width = column_class.shape[0]
    match = contract_class[:, None] == column_class[None, :]
    shaped = int_piece.reshape(tiles, P_SIZE, width, P_SIZE)
    kept = jnp.where(match[:, None, :, None], shaped, jnp.zeros_like(shaped)).reshape(
        count, width * P_SIZE
    )
    return jnp.dot(amp_piece, kept, preferred_element_type=jnp.float32)


def body(amplitudes, integrals, contract_class, column_class):
    slab = lax.all_gather(integrals, "occ", axis=0, tiled=True)
    return accumulate(
        lax.all_gather(amplitudes, "vir", axis=1, tiled=True), slab, contract_class, column_class
    )


def solution(mesh):
    placed = (P("occ", "vir"), P("occ", "vir"), P(), P("vir"))
    return jax.shard_map(
        body, mesh=mesh, in_specs=placed, out_specs=P("occ", "vir"), check_vma=False
    )
```

profile of v0, /device:TPU:1, one launch (start us, length us, event | category | flops | bytes accessed | tf_op | source)
XLA Modules:
  0.0 269.7 jit_solution(525118598297099982)
XLA Ops:
  6.5 0.0 all-gather.5.cloned.1.call-start
  6.5 0.7 all-gather.5.cloned.1.call-update
  7.3 0.0 all-gather.3.cloned.1.call-start
  7.3 0.7 all-gather.3.cloned.1.call-update
  8.0 0.7 broadcast_compare_fusion
  8.8 111.1 %all-gather.5.cloned.1.call-done = bf16[1024,2048]{1,0:T(8,128)(2,1)} async-done(((bf16[1024,128]{1,0:T(8,128)(2,1)}), bf16[1024,2048]{1,0:T(8,128)(2,1)}) %all-gather.5.cloned.1.call-update) | async-done | bytes 4194320 | tf_op jit(solution)/shard_map/all_gather | solution.py:24
  119.8 117.8 %all-gather.3.cloned.1.call-done = bf16[2048,2048]{1,0:T(8,128)(2,1)} async-done(((bf16[128,2048]{1,0:T(8,128)(2,1)}), bf16[2048,2048]{1,0:T(8,128)(2,1)}) %all-gather.3.cloned.1.call-update) | async-done | bytes 8388624 | tf_op jit(solution)/shard_map/all_gather | solution.py:22
  237.7 1.1 broadcast_in_dim.16
  238.8 15.0 %fusion.1 = f32[1024,2048]{0,1:T(8,128)} fusion(bf16[1024,2048]{1,0:T(8,128)(2,1)} %all-gather.5.cloned.1.call-done, bf16[2048,2048]{1,0:T(8,128)(2,1)} %all-gather.3.cloned.1.call-done, pred[256,8,16,128]{3,2,1,0:T(8,128)(4,1)S(1)} %bitcast.10), kind=kOutput, calls=%fused_computation.2 | convolution fusion | flops 8594128896 | bytes 25165824 | tf_op jit(solution)/shard_map/dot_general | solution.py:18
  253.8 9.1 %copy.5 = f32[1024,2048]{1,0:T(8,128)} copy(f32[1024,2048]{0,1:T(8,128)} %fusion.1) | data formatting | bytes 16777216 | tf_op jit(solution)/shard_map/dot_general | solution.py:18
Async XLA Ops:
  6.5 113.3 %all-gather.5.cloned.1.call-start = ((), (), s32[]{:S(2)}) async-start(), calls=%async_computation.1 | async-start | bytes 4456448 | tf_op jit(solution)/shard_map/all_gather | solution.py:24
  7.3 230.4 %all-gather.3.cloned.1.call-start = ((), (), s32[]{:S(2)}) async-start(), calls=%async_computation | async-start | bytes 8912896 | tf_op jit(solution)/shard_map/all_gather | solution.py:22
Sparse Core Ops, SparseCore 0:
  9.1 110.7 all-gather.4
  122.5 115.1 all-gather.2
where the time goes:
time: 270 us
  waiting for transfers between devices  230 us (85%)
  matrix products  15 us (6%)
  between operations  13.4 us (5%)
  local copies, waits for them, and re-layouts  10.3 us (4%)
    all_gather x1, waiting for transfers between devices, body(): slab = lax.all_gather(integrals, 'occ', axis=0, tiled=True)  118 us
    all_gather x1, waiting for transfers between devices, body(): lax.all_gather(amplitudes, 'vir', axis=1, tiled=True)  111 us
    dot_general x1, matrix products, accumulate(): return jnp.dot(amp_piece, kept, preferred_element_type=jnp.float32)  15 us
    dot_general x1, local copies, waits for them, and re-layouts, accumulate(): return jnp.dot(amp_piece, kept, preferred_element_type=jnp.float32)  9.12 us
  transfers between devices with their start and end apart: 2, of which 2 were waited for; matrix products, arithmetic and copies ran while one was open for 0% of the time, Pallas kernels for 0%

commit v1 on v0

v1 whole, which is shorter than its diff:
```python
import functools

import jax
import jax.numpy as jnp
from jax import lax
from jax.experimental import pallas as pl
from jax.experimental.pallas import tpu as pltpu
from jax.sharding import Mesh, PartitionSpec as P

P_SIZE = 128
OCC = ("x", "zh", "core")
VIR = ("y", "zl")
NY = 4
NZ = 4


def multiply_kernel(spots, slots, *refs):
    pieces, slab_ref = refs[: len(spots)], refs[len(spots)]
    out_ref, amps, sems = refs[len(spots) + 1 :]

    @pl.when(pl.program_id(0) == 0)
    def _():
        copies = [
            pltpu.make_async_copy(
                piece, amps.at[slot, pl.ds(start, piece.shape[0])], sems.at[i]
            )
            for i, (piece, (slot, start)) in enumerate(zip(pieces, spots))
        ]
        for copy in copies:
            copy.start()
        for copy in copies:
            copy.wait()

    l = pl.program_id(0)
    pair = jnp.concatenate([amps[slots[0, l]], amps[slots[1, l]]], axis=1)
    out_ref[...] = jnp.dot(pair, slab_ref[...], preferred_element_type=jnp.float32)


def multiply(slots, spots, pieces, slab):
    rows = pieces[0].shape[0]
    depth, width = slab.shape
    tiles = width // P_SIZE
    return pl.pallas_call(
        functools.partial(multiply_kernel, spots),
        out_shape=jax.ShapeDtypeStruct((rows, width), jnp.float32),
        grid_spec=pltpu.PrefetchScalarGridSpec(
            num_scalar_prefetch=1,
            grid=(tiles,),
            in_specs=[pl.BlockSpec(memory_space=pl.ANY)] * len(pieces)
            + [pl.BlockSpec((depth, P_SIZE), lambda l, slots: (0, l))],
            out_specs=pl.BlockSpec((rows, P_SIZE), lambda l, slots: (0, l)),
            scratch_shapes=[
                pltpu.VMEM((NY * NZ, rows, P_SIZE), jnp.bfloat16),
                pltpu.SemaphoreType.DMA((len(pieces),)),
            ],
        ),
        compiler_params=pltpu.CompilerParams(vmem_limit_bytes=32 * 1024 * 1024),
        cost_estimate=pl.CostEstimate(
            flops=2 * rows * depth * width,
            bytes_accessed=4 * rows * width + 2 * rows * P_SIZE * NY * NZ,
            transcendentals=0,
        ),
    )(slots, *pieces, slab)


def shift(value, axis, step, size):
    return lax.ppermute(value, axis, [(i, (i - step) % size) for i in range(size)])


def swap(value, axis, bit, size):
    return lax.ppermute(value, axis, [(i, i ^ bit) for i in range(size)])


def gather_pieces(own):
    half = own.shape[0] // 2
    line = [own] + [swap(own, "zl", bit, NZ) for bit in range(1, NZ)]
    spots, pieces = [], []
    for dz, block in enumerate(line):
        up = shift(block, "y", 1, NY)
        down = shift(block, "y", -1, NY)
        far_top = shift(up[:half], "y", 1, NY)
        far_bottom = shift(down[half:], "y", -1, NY)
        spots += [(dz, 0), (NZ + dz, 0), (3 * NZ + dz, 0)]
        spots += [(2 * NZ + dz, 0), (2 * NZ + dz, half)]
        pieces += [block, up, down, far_top, far_bottom]
    return tuple(spots), pieces


def body(amplitudes, integrals, contract_class, column_class):
    nk = contract_class.shape[0]
    me = lax.axis_index(OCC)
    y, z = lax.axis_index("y"), lax.axis_index("zl")

    same = contract_class[:, None] == contract_class[None, :]
    order = jnp.arange(nk, dtype=jnp.int32)
    rank = jnp.sum(same & (order[None, :] < order[:, None]), axis=1)
    mine, my_rank = contract_class[me], rank[me]
    hit = jnp.repeat(column_class == mine, P_SIZE)[None, None, :]
    place = (jnp.arange(2) == my_rank)[:, None, None]
    slab = jnp.where(hit & place, integrals[None], jnp.zeros_like(integrals)[None])
    slab = lax.psum(slab.reshape(2 * P_SIZE, -1), OCC)

    match = contract_class[None, :, None] == column_class[None, None, :]
    match = match & (rank[None, :, None] == jnp.arange(2)[:, None, None])
    slot = ((order // NZ - y) % NY) * NZ + ((order % NZ) ^ z)
    slots = jnp.sum(jnp.where(match, slot[None, :, None], 0), axis=1).astype(jnp.int32)

    spots, pieces = gather_pieces(amplitudes)
    return multiply(slots, spots, pieces, slab)


def solution(mesh):
    fine = Mesh(mesh.devices.reshape(4, 2, 2, NY, NZ), OCC + VIR)
    placed = (P(OCC, VIR), P(OCC, VIR), P(), P(VIR))
    return jax.shard_map(
        body, mesh=fine, in_specs=placed, out_specs=P(OCC, VIR), check_vma=False
    )
```

time: 270 us -> 226 us (0.84)
  waiting for transfers between devices: 230 us -> 160 us
  starting transfers between devices: 0.04 us -> 26.4 us
  matrix products: 15 us -> 0 us
  Pallas kernels: 0 us -> 11.7 us
  other arithmetic: 0.75 us -> 5.88 us
    all_gather x2 -> x0, waiting for transfers between devices: 229 us -> none  [the longest x1 118 us: body(): slab = lax.all_gather(integrals, 'occ', axis=0, tiled=True)]
    psum x0 -> x1, waiting for transfers between devices: none -> 136 us  [body(): slab = lax.psum(slab.reshape(2 * P_SIZE, -1), OCC)]
    ppermute x0 -> x19, starting transfers between devices: none -> 26.4 us  [the longest x16 20.8 us: shift(): lax.ppermute(value, axis, [(i, (i - step) % size) for i in range(size)])]
    ppermute x0 -> x19, waiting for transfers between devices: none -> 24 us  [the longest x3 12.1 us: swap(): return lax.ppermute(value, axis, [(i, i ^ bit) for i in range(size)])]
    dot_general x1 -> x0, matrix products: 15 us -> none  [accumulate(): return jnp.dot(amp_piece, kept, preferred_element_type=jnp.float32)]
    pallas_call x0 -> x1, Pallas kernels: none -> 11.7 us  [multiply(): pl.pallas_call(functools.partial(multiply_kernel, spots), out_shape=jax.S...]
    dot_general x1 -> x0, local copies, waits for them, and re-layouts: 9.12 us -> none  [accumulate(): return jnp.dot(amp_piece, kept, preferred_element_type=jnp.float32)]
    unnamed x0 -> x16, local copies, waits for them, and re-layouts: none -> 6.82 us
  transfers between devices with their start and end apart: 2 -> 20, of which waited for: 2 -> 9; matrix products, arithmetic and copies ran while one was open for 0% -> 3% of each run, Pallas kernels for 0% -> 0%
where the time goes in v1:
time: 226 us
  waiting for transfers between devices  160 us (71%)
  starting transfers between devices  26.4 us (12%)
  between operations  13.5 us (6%)
  Pallas kernels  11.7 us (5%)
  local copies, waits for them, and re-layouts  8.81 us (4%)
  other arithmetic  5.88 us (3%)
    psum x1, waiting for transfers between devices, body(): slab = lax.psum(slab.reshape(2 * P_SIZE, -1), OCC)  136 us
    ppermute x16, starting transfers between devices, shift(): lax.ppermute(value, axis, [(i, (i - step) % size) for i in range(size)])  20.8 us
    ppermute x3, waiting for transfers between devices, swap(): return lax.ppermute(value, axis, [(i, i ^ bit) for i in range(size)])  12.1 us
    ppermute x16, waiting for transfers between devices, shift(): lax.ppermute(value, axis, [(i, (i - step) % size) for i in range(size)])  11.9 us
    pallas_call x1, Pallas kernels, multiply(): pl.pallas_call(functools.partial(multiply_kernel, spots), out_shape=jax.S...  11.7 us
    unnamed x16, local copies, waits for them, and re-layouts  6.82 us
    ppermute x3, starting transfers between devices, swap(): return lax.ppermute(value, axis, [(i, i ^ bit) for i in range(size)])  5.55 us
  transfers between devices with their start and end apart: 20, of which 9 were waited for; matrix products, arithmetic and copies ran while one was open for 3% of the time, Pallas kernels for 0%

profile of v1, /device:TPU:1, one launch (start us, length us, event | category | flops | bytes accessed | tf_op | source)
XLA Modules:
  0.0 225.8 jit_solution(4486117170653925416)
XLA Ops:
  6.5 3.8 %collective-permute-start.9 = (bf16[1024,128]{1,0:T(8,128)(2,1)}, bf16[1024,128]{1,0:T(8,128)(2,1)S(1)}, u32[]{:S(2)}, u32[]{:S(2)}) collective-permute-start(bf16[1024,128]{1,0:T(8,128)(2,1)} %refs_0_.1), channel_id=1, source_target_pairs={{0,2},{1,3},{2,0},{3,1},{4,6},{5,7},{6,4},{7,5},{8,10},{9,11},{10,... | collective-permute-start | bytes 786440 | tf_op jit(solution)/shard_map/ppermute | solution.py:71
  10.4 0.9 convert_reduce_fusion
  11.3 1.2 dynamic_slice.6
  12.5 0.6 dynamic_slice.7
  13.1 0.6 iota_compare_fusion.2
  13.7 1.3 broadcast_compare_fusion.1
  15.1 0.1 broadcast_bitcast_fusion
  15.1 0.1 broadcast_and_fusion
  15.2 2.1 broadcast_select_fusion
  17.3 0.0 all-reduce.2.cloned.1.call-update
  17.3 1.7 collective-permute-start.4
  19.1 1.3 collective-permute-start.1
  20.4 1.4 collective-permute-start
  21.8 0.0 collective-permute-start.14
  21.8 0.0 collective-permute-done.9.refs_10_
  21.8 1.7 collective-permute-start.11
  23.5 12.1 %collective-permute-done.4.refs_5_ = bf16[1024,128]{1,0:T(8,128)(2,1)S(1)} collective-permute-done((bf16[1024,128]{1,0:T(8,128)(2,1)}, bf16[1024,128]{1,0:T(8,128)(2,1)S(1)}, u32[]{:S(2)}, u32[]{:S(2)}) %collective-permute-start.4) | collective-permute-done | bytes 262176 | tf_op jit(solution)/shard_map/ppermute | solution.py:71
  35.6 2.8 %collective-permute-start.10 = (bf16[1024,128]{1,0:T(8,128)(2,1)S(1)}, bf16[1024,128]{1,0:T(8,128)(2,1)S(1)}, u32[]{:S(2)}, u32[]{:S(2)}) collective-permute-start(bf16[1024,128]{1,0:T(8,128)(2,1)S(1)} %collective-permute-done.9.refs_10_), channel_id=1, source_target_pairs={{0,12},{4,0},{8,4},{12,8},{1,13},{5,1},{9,5},{13,9},{2,14},{6,2},{... | collective-permute-start | bytes 786440 | tf_op jit(solution)/shard_map/ppermute | solution.py:67
  38.4 0.0 collective-permute-done.refs_1_
  38.4 2.7 %collective-permute-start.5 = (bf16[1024,128]{1,0:T(8,128)(2,1)S(1)}, bf16[1024,128]{1,0:T(8,128)(2,1)S(1)}, u32[]{:S(2)}, u32[]{:S(2)}) collective-permute-start(bf16[1024,128]{1,0:T(8,128)(2,1)S(1)} %collective-permute-done.4.refs_5_), channel_id=1, source_target_pairs={{0,12},{4,0},{8,4},{12,8},{1,13},{5,1},{9,5},{13,9},{2,14},{6,2},{... | collective-permute-start | bytes 786440 | tf_op jit(solution)/shard_map/ppermute | solution.py:67
  41.1 2.7 %collective-permute-start.15 = (bf16[1024,128]{1,0:T(8,128)(2,1)S(1)}, bf16[1024,128]{1,0:T(8,128)(2,1)S(1)}, u32[]{:S(2)}, u32[]{:S(2)}) collective-permute-start(bf16[1024,128]{1,0:T(8,128)(2,1)S(1)} %collective-permute-done.14.refs_15_), channel_id=1, source_target_pairs={{0,12},{4,0},{8,4},{12,8},{1,13},{5,1},{9,5},{13,9},{2,14},{6,2},{... | collective-permute-start | bytes 786440 | tf_op jit(solution)/shard_map/ppermute | solution.py:67
  43.8 0.7 broadcast_compare_fusion
  44.6 0.0 collective-permute-done.10.refs_11_
  44.6 0.1 collective-permute-start.3
  44.7 2.1 collective-permute-done.6.refs_7_
  46.8 0.5 collective-permute-start.2
  47.4 2.0 collective-permute-done.5.refs_6_
  49.3 0.6 collective-permute-start.13
  50.1 2.4 %collective-permute-done.16.refs_17_ = bf16[1024,128]{1,0:T(8,128)(2,1)S(1)} collective-permute-done((bf16[1024,128]{1,0:T(8,128)(2,1)S(1)}, bf16[1024,128]{1,0:T(8,128)(2,1)S(1)}, u32[]{:S(2)}, u32[]{:S(2)}) %collective-permute-start.16) | collective-permute-done | bytes 262176 | tf_op jit(solution)/shard_map/ppermute | solution.py:67
  52.5 0.5 collective-permute-start.12
  53.0 1.9 collective-permute-done.15.refs_16_
  55.0 0.5 collective-permute-start.8
  55.5 3.1 %collective-permute-start.7 = (bf16[512,128]{1,0:T(8,128)(2,1)S(1)}, bf16[512,128]{1,0:T(8,128)(2,1)S(1)}, u32[]{:S(2)}, u32[]{:S(2)}) collective-permute-start(bf16[512,128]{1,0:T(8,128)(2,1)S(1)} %slice.34), channel_id=1, source_target_pairs={{0,12},{4,0},{8,4},{12,8},{1,13},{5,1},{9,5},{13,9},{2,14},{6,2},{... | collective-permute-start | bytes 393224 | tf_op jit(solution)/shard_map/ppermute | solution.py:67
  58.7 2.7 %collective-permute-start.17 = (bf16[512,128]{1,0:T(8,128)(2,1)S(1)}, bf16[512,128]{1,0:T(8,128)(2,1)S(1)}, u32[]{:S(2)}, u32[]{:S(2)}) collective-permute-start(bf16[512,128]{1,0:T(8,128)(2,1)S(1)} %slice.38), channel_id=1, source_target_pairs={{0,12},{4,0},{8,4},{12,8},{1,13},{5,1},{9,5},{13,9},{2,14},{6,2},{... | collective-permute-start | bytes 393224 | tf_op jit(solution)/shard_map/ppermute | solution.py:67
  61.4 0.1 select_reduce_fusion.slots
  61.5 1.9 collective-permute-done.7.refs_8_
  63.4 0.6 copy-done.2
  64.0 0.3 collective-permute-done.18.refs_19_
  64.4 0.6 copy-done.4
  65.0 1.2 collective-permute-done.17.refs_18_
  66.2 0.6 copy-done.6
  66.8 135.6 %all-reduce.2.cloned.1.call-done.refs_20_ = bf16[256,2048]{1,0:T(8,128)(2,1)} async-done(((bf16[256,2048]{1,0:T(8,128)(2,1)}), bf16[256,2048]{1,0:T(8,128)(2,1)}) %all-reduce.2.cloned.1.call-update) | async-done | bytes 1048592 | tf_op jit(solution)/shard_map/psum | solution.py:101
  202.4 1.2 copy-done
  203.6 0.9 copy-done.1
  204.6 0.9 copy-done.3
  205.5 0.9 copy-done.5
  206.4 0.9 copy-done.7
  207.3 11.7 %shard_map.46 = f32[1024,2048]{1,0:T(8,128)} custom-call(s32[2,16]{1,0:T(2,128)S(1)} %select_reduce_fusion.slots, bf16[1024,128]{1,0:T(8,128)(2,1)S(1)} %copy-done.1, bf16[1024,128]{1,0:T(8,128)(2,1)S(1)} %collective-permute-done.refs_1_, bf16[1024,128]{1,0:T(8,128)(2,1)S(1)} %collective-permute-done.1.refs_2_, ...), custom_call_target="tpu_custom_call" | custom-call | flops 1073741824 | bytes 12582912 | tf_op jit(solution)/shard_map/pallas_call | solution.py:43
  (30 shorter events, 0.1 us)
Async XLA Ops:
  6.5 195.9 %all-reduce.2.cloned.1.call-start = ((), (), s32[]{:S(2)}) async-start(), calls=%async_computation | async-start | bytes 2097152 | tf_op jit(solution)/shard_map/psum | solution.py:101
  6.5 15.3 %collective-permute-start.9 = (bf16[1024,128]{1,0:T(8,128)(2,1)}, bf16[1024,128]{1,0:T(8,128)(2,1)S(1)}, u32[]{:S(2)}, u32[]{:S(2)}) collective-permute-start(bf16[1024,128]{1,0:T(8,128)(2,1)} %refs_0_.1), channel_id=1, source_target_pairs={{0,2},{1,3},{2,0},{3,1},{4,6},{5,7},{6,4},{7,5},{8,10},{9,11},{10,... | collective-permute-start | bytes 786440 | tf_op jit(solution)/shard_map/ppermute | solution.py:71
  17.3 18.3 %collective-permute-start.4 = (bf16[1024,128]{1,0:T(8,128)(2,1)}, bf16[1024,128]{1,0:T(8,128)(2,1)S(1)}, u32[]{:S(2)}, u32[]{:S(2)}) collective-permute-start(bf16[1024,128]{1,0:T(8,128)(2,1)} %refs_0_.1), channel_id=1, source_target_pairs={{0,1},{1,0},{2,3},{3,2},{4,5},{5,4},{6,7},{7,6},{8,9},{9,8},{10,11... | collective-permute-start | bytes 786440 | tf_op jit(solution)/shard_map/ppermute | solution.py:71
  19.1 19.4 %collective-permute-start.1 = (bf16[1024,128]{1,0:T(8,128)(2,1)}, bf16[1024,128]{1,0:T(8,128)(2,1)S(1)}, u32[]{:S(2)}, u32[]{:S(2)}) collective-permute-start(bf16[1024,128]{1,0:T(8,128)(2,1)} %refs_0_.1), channel_id=1, source_target_pairs={{0,4},{4,8},{8,12},{12,0},{1,5},{5,9},{9,13},{13,1},{2,6},{6,10},{... | collective-permute-start | bytes 786440 | tf_op jit(solution)/shard_map/ppermute | solution.py:67
  20.4 18.1 %collective-permute-start = (bf16[1024,128]{1,0:T(8,128)(2,1)}, bf16[1024,128]{1,0:T(8,128)(2,1)S(1)}, u32[]{:S(2)}, u32[]{:S(2)}) collective-permute-start(bf16[1024,128]{1,0:T(8,128)(2,1)} %refs_0_.1), channel_id=1, source_target_pairs={{0,12},{4,0},{8,4},{12,8},{1,13},{5,1},{9,5},{13,9},{2,14},{6,2},{... | collective-permute-start | bytes 786440 | tf_op jit(solution)/shard_map/ppermute | solution.py:67
  21.8 19.3 %collective-permute-start.14 = (bf16[1024,128]{1,0:T(8,128)(2,1)}, bf16[1024,128]{1,0:T(8,128)(2,1)S(1)}, u32[]{:S(2)}, u32[]{:S(2)}) collective-permute-start(bf16[1024,128]{1,0:T(8,128)(2,1)} %refs_0_.1), channel_id=1, source_target_pairs={{0,3},{1,2},{2,1},{3,0},{4,7},{5,6},{6,5},{7,4},{8,11},{9,10},{10,... | collective-permute-start | bytes 786440 | tf_op jit(solution)/shard_map/ppermute | solution.py:71
  21.8 19.3 %collective-permute-start.11 = (bf16[1024,128]{1,0:T(8,128)(2,1)S(1)}, bf16[1024,128]{1,0:T(8,128)(2,1)S(1)}, u32[]{:S(2)}, u32[]{:S(2)}) collective-permute-start(bf16[1024,128]{1,0:T(8,128)(2,1)S(1)} %collective-permute-done.9.refs_10_), channel_id=1, source_target_pairs={{0,4},{4,8},{8,12},{12,0},{1,5},{5,9},{9,13},{13,1},{2,6},{6,10},{... | collective-permute-start | bytes 786440 | tf_op jit(solution)/shard_map/ppermute | solution.py:67
  35.6 9.0 %collective-permute-start.10 = (bf16[1024,128]{1,0:T(8,128)(2,1)S(1)}, bf16[1024,128]{1,0:T(8,128)(2,1)S(1)}, u32[]{:S(2)}, u32[]{:S(2)}) collective-permute-start(bf16[1024,128]{1,0:T(8,128)(2,1)S(1)} %collective-permute-done.9.refs_10_), channel_id=1, source_target_pairs={{0,12},{4,0},{8,4},{12,8},{1,13},{5,1},{9,5},{13,9},{2,14},{6,2},{... | collective-permute-start | bytes 786440 | tf_op jit(solution)/shard_map/ppermute | solution.py:67
  38.4 8.4 %collective-permute-start.6 = (bf16[1024,128]{1,0:T(8,128)(2,1)S(1)}, bf16[1024,128]{1,0:T(8,128)(2,1)S(1)}, u32[]{:S(2)}, u32[]{:S(2)}) collective-permute-start(bf16[1024,128]{1,0:T(8,128)(2,1)S(1)} %collective-permute-done.4.refs_5_), channel_id=1, source_target_pairs={{0,4},{4,8},{8,12},{12,0},{1,5},{5,9},{9,13},{13,1},{2,6},{6,10},{... | collective-permute-start | bytes 786440 | tf_op jit(solution)/shard_map/ppermute | solution.py:67
  38.4 10.9 %collective-permute-start.5 = (bf16[1024,128]{1,0:T(8,128)(2,1)S(1)}, bf16[1024,128]{1,0:T(8,128)(2,1)S(1)}, u32[]{:S(2)}, u32[]{:S(2)}) collective-permute-start(bf16[1024,128]{1,0:T(8,128)(2,1)S(1)} %collective-permute-done.4.refs_5_), channel_id=1, source_target_pairs={{0,12},{4,0},{8,4},{12,8},{1,13},{5,1},{9,5},{13,9},{2,14},{6,2},{... | collective-permute-start | bytes 786440 | tf_op jit(solution)/shard_map/ppermute | solution.py:67
  41.1 11.4 %collective-permute-start.16 = (bf16[1024,128]{1,0:T(8,128)(2,1)S(1)}, bf16[1024,128]{1,0:T(8,128)(2,1)S(1)}, u32[]{:S(2)}, u32[]{:S(2)}) collective-permute-start(bf16[1024,128]{1,0:T(8,128)(2,1)S(1)} %collective-permute-done.14.refs_15_), channel_id=1, source_target_pairs={{0,4},{4,8},{8,12},{12,0},{1,5},{5,9},{9,13},{13,1},{2,6},{6,10},{... | collective-permute-start | bytes 786440 | tf_op jit(solution)/shard_map/ppermute | solution.py:67
  41.1 13.8 %collective-permute-start.15 = (bf16[1024,128]{1,0:T(8,128)(2,1)S(1)}, bf16[1024,128]{1,0:T(8,128)(2,1)S(1)}, u32[]{:S(2)}, u32[]{:S(2)}) collective-permute-start(bf16[1024,128]{1,0:T(8,128)(2,1)S(1)} %collective-permute-done.14.refs_15_), channel_id=1, source_target_pairs={{0,12},{4,0},{8,4},{12,8},{1,13},{5,1},{9,5},{13,9},{2,14},{6,2},{... | collective-permute-start | bytes 786440 | tf_op jit(solution)/shard_map/ppermute | solution.py:67
  44.6 10.9 %collective-permute-start.3 = (bf16[512,128]{1,0:T(8,128)(2,1)S(1)}, bf16[512,128]{1,0:T(8,128)(2,1)S(1)}, u32[]{:S(2)}, u32[]{:S(2)}) collective-permute-start(bf16[512,128]{1,0:T(8,128)(2,1)S(1)} %slice.33), channel_id=1, source_target_pairs={{0,4},{4,8},{8,12},{12,0},{1,5},{5,9},{9,13},{13,1},{2,6},{6,10},{... | collective-permute-start | bytes 393224 | tf_op jit(solution)/shard_map/ppermute | solution.py:67
  46.8 11.8 %collective-permute-start.2 = (bf16[512,128]{1,0:T(8,128)(2,1)S(1)}, bf16[512,128]{1,0:T(8,128)(2,1)S(1)}, u32[]{:S(2)}, u32[]{:S(2)}) collective-permute-start(bf16[512,128]{1,0:T(8,128)(2,1)S(1)} %slice.32), channel_id=1, source_target_pairs={{0,12},{4,0},{8,4},{12,8},{1,13},{5,1},{9,5},{13,9},{2,14},{6,2},{... | collective-permute-start | bytes 393224 | tf_op jit(solution)/shard_map/ppermute | solution.py:67
  49.3 9.3 %collective-permute-start.13 = (bf16[512,128]{1,0:T(8,128)(2,1)S(1)}, bf16[512,128]{1,0:T(8,128)(2,1)S(1)}, u32[]{:S(2)}, u32[]{:S(2)}) collective-permute-start(bf16[512,128]{1,0:T(8,128)(2,1)S(1)} %slice.37), channel_id=1, source_target_pairs={{0,4},{4,8},{8,12},{12,0},{1,5},{5,9},{9,13},{13,1},{2,6},{6,10},{... | collective-permute-start | bytes 393224 | tf_op jit(solution)/shard_map/ppermute | solution.py:67
  52.5 9.0 %collective-permute-start.12 = (bf16[512,128]{1,0:T(8,128)(2,1)S(1)}, bf16[512,128]{1,0:T(8,128)(2,1)S(1)}, u32[]{:S(2)}, u32[]{:S(2)}) collective-permute-start(bf16[512,128]{1,0:T(8,128)(2,1)S(1)} %slice.36), channel_id=1, source_target_pairs={{0,12},{4,0},{8,4},{12,8},{1,13},{5,1},{9,5},{13,9},{2,14},{6,2},{... | collective-permute-start | bytes 393224 | tf_op jit(solution)/shard_map/ppermute | solution.py:67
  55.0 6.5 %collective-permute-start.8 = (bf16[512,128]{1,0:T(8,128)(2,1)S(1)}, bf16[512,128]{1,0:T(8,128)(2,1)S(1)}, u32[]{:S(2)}, u32[]{:S(2)}) collective-permute-start(bf16[512,128]{1,0:T(8,128)(2,1)S(1)} %slice.35), channel_id=1, source_target_pairs={{0,4},{4,8},{8,12},{12,0},{1,5},{5,9},{9,13},{13,1},{2,6},{6,10},{... | collective-permute-start | bytes 393224 | tf_op jit(solution)/shard_map/ppermute | solution.py:67
  55.5 7.9 %collective-permute-start.7 = (bf16[512,128]{1,0:T(8,128)(2,1)S(1)}, bf16[512,128]{1,0:T(8,128)(2,1)S(1)}, u32[]{:S(2)}, u32[]{:S(2)}) collective-permute-start(bf16[512,128]{1,0:T(8,128)(2,1)S(1)} %slice.34), channel_id=1, source_target_pairs={{0,12},{4,0},{8,4},{12,8},{1,13},{5,1},{9,5},{13,9},{2,14},{6,2},{... | collective-permute-start | bytes 393224 | tf_op jit(solution)/shard_map/ppermute | solution.py:67
  58.7 5.7 %collective-permute-start.18 = (bf16[512,128]{1,0:T(8,128)(2,1)S(1)}, bf16[512,128]{1,0:T(8,128)(2,1)S(1)}, u32[]{:S(2)}, u32[]{:S(2)}) collective-permute-start(bf16[512,128]{1,0:T(8,128)(2,1)S(1)} %slice.39), channel_id=1, source_target_pairs={{0,4},{4,8},{8,12},{12,0},{1,5},{5,9},{9,13},{13,1},{2,6},{6,10},{... | collective-permute-start | bytes 393224 | tf_op jit(solution)/shard_map/ppermute | solution.py:67
  58.7 7.5 %collective-permute-start.17 = (bf16[512,128]{1,0:T(8,128)(2,1)S(1)}, bf16[512,128]{1,0:T(8,128)(2,1)S(1)}, u32[]{:S(2)}, u32[]{:S(2)}) collective-permute-start(bf16[512,128]{1,0:T(8,128)(2,1)S(1)} %slice.38), channel_id=1, source_target_pairs={{0,12},{4,0},{8,4},{12,8},{1,13},{5,1},{9,5},{13,9},{2,14},{6,2},{... | collective-permute-start | bytes 393224 | tf_op jit(solution)/shard_map/ppermute | solution.py:67
  63.4 0.7 copy-start.2
  64.4 0.6 copy-start.4
  66.2 0.6 copy-start.6
  202.4 1.2 copy-start
  203.6 0.9 copy-start.1
  204.6 0.9 copy-start.3
  205.5 0.9 copy-start.5
  206.4 0.9 copy-start.7
Sparse Core Ops, SparseCore 0:
  17.4 184.9 all-reduce.1

commit v2 on v0

v2 whole, which is shorter than its diff:
```python
import functools

import jax
import jax.numpy as jnp
from jax import lax
from jax.experimental import pallas as pl
from jax.experimental.pallas import tpu as pltpu
from jax.sharding import Mesh, PartitionSpec as P

P_SIZE = 128
SYMS = 8
OCC = ("x", "zh", "core")
VIR = ("y", "zl")
NX = NY = NZ = 4
NK = 16
QUARTER = 4
STEP = 256

SLOTS = 0
MERGE = 2 * NK
HALVES = MERGE + 2 * QUARTER
TABLE = HALVES + 2 * QUARTER

VMEM = pl.BlockSpec(memory_space=pltpu.VMEM)
SMEM = pl.BlockSpec(memory_space=pltpu.SMEM)
ANY = pl.BlockSpec(memory_space=pl.ANY)


def swap_cores(value):
    return lax.ppermute(value, "core", [(0, 1), (1, 0)])


def ring(value):
    pairs = []
    for y in range(NY):
        pairs += [(y, (y + 1) % NY), (NY + y, NY + (y - 1) % NY)]
    return lax.ppermute(value, ("core", "y"), pairs)


def cross_x(value, bits):
    pairs = [(2 * x + c, 2 * (x ^ bits[c]) + c) for x in range(NX) for c in range(2)]
    return lax.ppermute(value, ("x", "core"), pairs)


def cross_z(value, bits):
    pairs = [(NZ * c + z, NZ * c + (z ^ bits[c])) for z in range(NZ) for c in range(2)]
    return lax.ppermute(value, ("core", "zl"), pairs)


def table_kernel(contract, column, out, inverse, rank, chosen):
    x, zh, c = (lax.axis_index(axis) for axis in OCC)
    y, z = (lax.axis_index(axis) for axis in VIR)
    one, two = (y + 3 + 2 * c) % NY, (y + 1 + 2 * c) % NY
    far = (y + 2) % NY
    near, other = z ^ (1 + c), z ^ (2 - c)
    sources = [
        (y, z), (y, near), (y, other), (y, z ^ 3),
        (one, z), (two, z), (far, z),
        (one, near), (two, other), (one, other), (two, near),
        (one, z ^ 3), (two, z ^ 3),
        (far, z ^ 1), (far, z ^ 2), (far, z ^ 3),
    ]
    for i, (row, col) in enumerate(sources):
        inverse[row * NZ + col] = i
    for s in range(SYMS):
        chosen[2 * SYMS + s] = 0
    for k in range(NK):
        label = contract[k]
        place = chosen[2 * SYMS + label]
        rank[k] = place
        chosen[2 * label + place] = inverse[k]
        chosen[2 * SYMS + label] = place + 1
    for l in range(NK):
        for r in range(2):
            out[SLOTS + r * NK + l] = chosen[2 * column[l] + r]

    near_x = x ^ (1 + 2 * c)
    tiles = [
        x * 4 + zh * 2 + c,
        near_x * 4 + zh * 2 + c,
        near_x * 4 + zh * 2 + 1 - c,
        (x ^ 2) * 4 + zh * 2 + c,
    ]
    for j in range(QUARTER):
        half = c if j < 2 else 1 - c
        label = column[QUARTER * x + 2 * half + j % 2]
        for r in range(2):
            found = jnp.int32(len(tiles))
            for s, tile in enumerate(tiles):
                hit = (contract[tile] == label) & (rank[tile] == r)
                found = jnp.where(hit, s, found)
            out[MERGE + r * QUARTER + j] = found

    far_x = x ^ (3 - 2 * c)
    halves = [
        (x, c), (x, 1 - c),
        (near_x, c), (near_x, 1 - c),
        (far_x, 1 - c), (far_x, c),
        (x ^ 2, c), (x ^ 2, 1 - c),
    ]
    for i, (quarter, half) in enumerate(halves):
        out[HALVES + 2 * quarter + half] = i


def make_table(contract_class, column_class):
    return pl.pallas_call(
        table_kernel,
        out_shape=jax.ShapeDtypeStruct((TABLE,), jnp.int32),
        in_specs=[SMEM, SMEM],
        out_specs=SMEM,
        scratch_shapes=[
            pltpu.SMEM((NK,), jnp.int32),
            pltpu.SMEM((NK,), jnp.int32),
            pltpu.SMEM((3 * SYMS,), jnp.int32),
        ],
    )(contract_class, column_class)


def cut_kernel(integrals, own, near, far, across, sems):
    x, c = lax.axis_index("x"), lax.axis_index("core")
    width = own.shape[1]
    quarters = [x, x ^ (1 + 2 * c), x ^ (3 - 2 * c), x ^ 2]
    copies = []
    for i, (quarter, out) in enumerate(zip(quarters, (own, near, far, across))):
        columns = pl.ds(pl.multiple_of(quarter * width, width), width)
        copies.append(pltpu.make_async_copy(integrals.at[:, columns], out, sems.at[i]))
    for copy in copies:
        copy.start()
    for copy in copies:
        copy.wait()


def cut(integrals):
    depth, width = integrals.shape
    shape = jax.ShapeDtypeStruct((depth, width // NX), integrals.dtype)
    return pl.pallas_call(
        cut_kernel,
        out_shape=[shape] * 4,
        in_specs=[ANY],
        out_specs=[VMEM] * 4,
        scratch_shapes=[pltpu.SemaphoreType.DMA((4,))],
    )(integrals)


def merge_kernel(table, own, near, across, keep, send):
    tiles = [own, near.at[:P_SIZE], near.at[P_SIZE:], across]
    c = lax.axis_index("core")
    for j in range(QUARTER):
        half = c if j < 2 else 1 - c
        start = pl.multiple_of((2 * half + j % 2) * P_SIZE, P_SIZE)
        values = [tile[:, pl.ds(start, P_SIZE)] for tile in tiles]
        out = keep if j < 2 else send
        for r in range(2):
            found = table[MERGE + r * QUARTER + j]
            total = jnp.zeros_like(values[0])
            for s, value in enumerate(values):
                total = jnp.where(found == s, value, total)
            lane = (j % 2) * P_SIZE
            out[r * P_SIZE : (r + 1) * P_SIZE, lane : lane + P_SIZE] = total


def merge(table, own, near, across):
    shape = jax.ShapeDtypeStruct((2 * P_SIZE, 2 * P_SIZE), own.dtype)
    return pl.pallas_call(
        merge_kernel,
        out_shape=[shape] * 2,
        in_specs=[SMEM, VMEM, VMEM, VMEM],
        out_specs=[VMEM] * 2,
    )(table, own, near, across)


def make_slab(integrals, table):
    own, near, far, across = cut(integrals)
    near = jnp.concatenate([near, swap_cores(far)])
    near = cross_x(near, (1, 3))
    across = cross_x(across, (2, 2))
    keep, send = merge(table, own, near, across)
    part = keep + swap_cores(send)
    part = part + lax.ppermute(part, "zh", [(0, 1), (1, 0)])
    pair = jnp.concatenate([part, swap_cores(part)])
    near = cross_x(pair, (1, 3))
    across = cross_x(part, (2, 2))
    return [pair, near, swap_cores(near), across, swap_cores(across)]


def gather_amplitudes(own):
    rows = own.shape[0]
    pair = jnp.concatenate([own, swap_cores(own)])
    line = cross_z(pair, (1, 2))
    up0 = ring(pair)
    turned = swap_cores(line)
    up1 = ring(line)
    last = cross_z(line[:rows], (2, 1))
    far0 = ring(up0[:rows])
    up2 = ring(turned)
    up3 = ring(jnp.concatenate([last, swap_cores(last)]))
    far1 = cross_z(far0, (1, 1))
    far2 = cross_z(far0, (2, 2))
    far3 = ring(up3[:rows])
    down0 = swap_cores(up0[rows:])
    down1 = swap_cores(up1[rows:])
    down2 = swap_cores(up2[:rows])
    down3 = swap_cores(up3[rows:])
    return [
        (own, 0), (line, 0), (turned, rows), (last, 0),
        (up0, 0), (down0, 0), (far0, 0),
        (up1, 0), (down1, 0), (up2, rows), (down2, 0),
        (up3, 0), (down3, 0),
        (far1, 0), (far2, 0), (far3, 0),
    ]


def multiply_kernel(starts, table, *refs):
    pieces, refs = refs[:NK], refs[NK:]
    parts, (out, amps, slab, sems) = refs[:5], refs[5:]
    rows = amps.shape[1]

    @pl.when(pl.program_id(0) == 0)
    def _():
        copies = []
        for i, (piece, start) in enumerate(zip(pieces, starts)):
            source = piece.at[pl.ds(start, rows)]
            copies.append(pltpu.make_async_copy(source, amps.at[i], sems.at[i]))
        place = 0
        for i, part in enumerate(parts):
            size = part.shape[0]
            target = slab.at[pl.ds(place, size)]
            copies.append(pltpu.make_async_copy(part, target, sems.at[NK + i]))
            place += size
        for copy in copies:
            copy.start()
        for copy in copies:
            copy.wait()

    block = pl.ds(pl.multiple_of(pl.program_id(0) * STEP, STEP), STEP)
    depth = 2 * P_SIZE
    for l in range(NK):
        pair = jnp.concatenate(
            [amps[table[SLOTS + r * NK + l], block] for r in range(2)], axis=1
        )
        place = pl.multiple_of(table[HALVES + l // 2] * depth, depth)
        lane = (l % 2) * P_SIZE
        weights = slab[pl.ds(place, depth), lane : lane + P_SIZE]
        out[:, l * P_SIZE : (l + 1) * P_SIZE] = jnp.dot(
            pair, weights, preferred_element_type=jnp.float32
        )


def multiply(table, pieces, parts):
    rows = pieces[0][0].shape[0]
    width = NK * P_SIZE
    starts = tuple(start for _, start in pieces)
    return pl.pallas_call(
        functools.partial(multiply_kernel, starts),
        out_shape=jax.ShapeDtypeStruct((rows, width), jnp.float32),
        grid_spec=pltpu.PrefetchScalarGridSpec(
            num_scalar_prefetch=1,
            grid=(rows // STEP,),
            in_specs=[ANY] * (NK + len(parts)),
            out_specs=pl.BlockSpec((STEP, width), lambda i, table: (i, 0)),
            scratch_shapes=[
                pltpu.VMEM((NK, rows, P_SIZE), jnp.bfloat16),
                pltpu.VMEM((2 * NK * P_SIZE // 2, 2 * P_SIZE), jnp.bfloat16),
                pltpu.SemaphoreType.DMA((NK + len(parts),)),
            ],
        ),
        compiler_params=pltpu.CompilerParams(vmem_limit_bytes=24 * 1024 * 1024),
        cost_estimate=pl.CostEstimate(
            flops=4 * rows * P_SIZE * width,
            bytes_accessed=4 * rows * width,
            transcendentals=0,
        ),
    )(table, *[piece for piece, _ in pieces], *parts)


def body(amplitudes, integrals, contract_class, column_class):
    table = make_table(contract_class, column_class)
    pieces = gather_amplitudes(amplitudes)
    parts = make_slab(integrals, table)
    return multiply(table, pieces, parts)


def solution(mesh):
    fine = Mesh(mesh.devices.reshape(NX, 2, 2, NY, NZ), OCC + VIR)
    placed = (P(OCC, VIR), P(OCC, VIR), P(), P(VIR))
    return jax.shard_map(
        body, mesh=fine, in_specs=placed, out_specs=P(OCC, VIR), check_vma=False
    )
```

time: 270 us -> 96.3 us (0.36)
  waiting for transfers between devices: 230 us -> 39.8 us
  starting transfers between devices: 0.04 us -> 40 us
  matrix products: 15 us -> 0 us
  between operations: 13.4 us -> 0.34 us
  Pallas kernels: 0 us -> 11.4 us
  local copies, waits for them, and re-layouts: 10.3 us -> 2.51 us
    all_gather x2 -> x0, waiting for transfers between devices: 229 us -> none  [the longest x1 118 us: body(): slab = lax.all_gather(integrals, 'occ', axis=0, tiled=True)]
    ppermute x0 -> x27, starting transfers between devices: none -> 40 us  [the longest x12 11.8 us: swap_cores(): return lax.ppermute(value, 'core', [(0, 1), (1, 0)])]
    ppermute x0 -> x27, waiting for transfers between devices: none -> 39.8 us  [the longest x4 15.3 us: cross_z(): return lax.ppermute(value, ('core', 'zl'), pairs)]
    dot_general x1 -> x0, matrix products: 15 us -> none  [accumulate(): return jnp.dot(amp_piece, kept, preferred_element_type=jnp.float32)]
    pallas_call x0 -> x4, Pallas kernels: none -> 11.4 us  [the longest x1 6.22 us: multiply(): pl.pallas_call(functools.partial(multiply_kernel, starts), out_shape=jax....]
    dot_general x1 -> x0, local copies, waits for them, and re-layouts: 9.12 us -> none  [accumulate(): return jnp.dot(amp_piece, kept, preferred_element_type=jnp.float32)]
  transfers between devices with their start and end apart: 2 -> 27, of which waited for: 2 -> 9; matrix products, arithmetic and copies ran while one was open for 0% -> 3% of each run, Pallas kernels for 0% -> 5%
where the time goes in v2:
time: 96.3 us; the launch traced here: 96.1 us
  starting transfers between devices  40 us (42%)
  waiting for transfers between devices  39.8 us (41%)
  Pallas kernels  11.4 us (12%)
  local copies, waits for them, and re-layouts  2.51 us (3%)
  other arithmetic  1.95 us (2%)
    ppermute x4, waiting for transfers between devices, cross_z(): return lax.ppermute(value, ('core', 'zl'), pairs)  15.3 us
    ppermute x6, waiting for transfers between devices, ring(): return lax.ppermute(value, ('core', 'y'), pairs)  12.4 us
    ppermute x12, starting transfers between devices, swap_cores(): return lax.ppermute(value, 'core', [(0, 1), (1, 0)])  11.8 us
    ppermute x4, starting transfers between devices, cross_x(): return lax.ppermute(value, ('x', 'core'), pairs)  9 us
    ppermute x6, starting transfers between devices, ring(): return lax.ppermute(value, ('core', 'y'), pairs)  7.55 us
    pallas_call x1, Pallas kernels, multiply(): pl.pallas_call(functools.partial(multiply_kernel, starts), out_shape=jax....  6.22 us
    ppermute x4, starting transfers between devices, cross_z(): return lax.ppermute(value, ('core', 'zl'), pairs)  6.18 us
    ppermute x1, starting transfers between devices, make_slab(): part = part + lax.ppermute(part, 'zh', [(0, 1), (1, 0)])  5.47 us
  transfers between devices with their start and end apart: 27, of which 9 were waited for; matrix products, arithmetic and copies ran while one was open for 3% of the time, Pallas kernels for 5%

profile of v2, /device:TPU:1, one launch (start us, length us, event | category | flops | bytes accessed | tf_op | source)
XLA Modules:
  0.0 96.1 jit_solution(3264421941018619020)
XLA Ops:
  0.0 3.2 %collective-permute-start = (bf16[1024,128]{1,0:T(8,128)(2,1)}, bf16[1024,128]{1,0:T(8,128)(2,1)S(1)}, u32[]{:S(2)}, u32[]{:S(2)}) collective-permute-start(bf16[1024,128]{1,0:T(8,128)(2,1)} %refs_0_.1), channel_id=1, source_target_pairs={{0,16},{16,0},{1,17},{17,1},{2,18},{18,2},{3,19},{19,3},{4,20},{20... | collective-permute-start | bytes 786440 | tf_op jit(solution)/shard_map/ppermute | solution.py:30
  3.2 1.0 %constant_dynamic-update-slice_fusion.1 = bf16[2048,128]{1,0:T(8,128)(2,1)S(1)} fusion(bf16[1024,128]{1,0:T(8,128)(2,1)} %refs_0_.1), kind=kLoop, calls=%fused_computation.4 | loop fusion | bytes 524288
  4.2 0.4 collective-permute-done
  4.7 1.3 %collective-permute-start.1 = (bf16[2048,128]{1,0:T(8,128)(2,1)S(1)}, bf16[2048,128]{1,0:T(8,128)(2,1)S(1)}, u32[]{:S(2)}, u32[]{:S(2)}) collective-permute-start(bf16[2048,128]{1,0:T(8,128)(2,1)S(1)} %constant_dynamic-update-slice_fusion), channel_id=1, source_target_pairs={{0,1},{16,18},{1,0},{17,19},{2,3},{18,16},{3,2},{19,17},{4,5},{20,... | collective-permute-start | bytes 1572872 | tf_op jit(solution)/shard_map/ppermute | solution.py:47
  6.0 1.9 %shard_map.47 = (bf16[128,512]{1,0:T(8,128)(2,1)}, bf16[128,512]{1,0:T(8,128)(2,1)}, bf16[128,512]{1,0:T(8,128)(2,1)}, bf16[128,512]{1,0:T(8,128)(2,1)}) custom-call(bf16[128,2048]{1,0:T(8,128)(2,1)} %integrals.1), custom_call_target="tpu_custom_call" | custom-call | tf_op jit(solution)/shard_map/pallas_call | solution.py:136
  7.9 0.1 collective-permute-start.17
  8.0 1.5 %collective-permute-done.17 = bf16[128,512]{1,0:T(8,128)(2,1)S(1)} collective-permute-done((bf16[128,512]{1,0:T(8,128)(2,1)}, bf16[128,512]{1,0:T(8,128)(2,1)S(1)}, u32[]{:S(2)}, u32[]{:S(2)}) %collective-permute-start.17) | collective-permute-done | bytes 131104 | tf_op jit(solution)/shard_map/ppermute | solution.py:30
  9.6 0.9 pad_maximum_fusion.1
  10.5 2.6 %collective-permute-start.18 = (bf16[256,512]{1,0:T(8,128)(2,1)S(1)}, bf16[256,512]{1,0:T(8,128)(2,1)S(1)}, u32[]{:S(2)}, u32[]{:S(2)}) collective-permute-start(bf16[256,512]{1,0:T(8,128)(2,1)S(1)} %pad_maximum_fusion.1), channel_id=1, source_target_pairs={{0,64},{16,208},{64,0},{80,144},{128,192},{144,80},{192,128},{208,... | collective-permute-start | bytes 786440 | tf_op jit(solution)/shard_map/ppermute | solution.py:42
  13.1 6.2 %collective-permute-done.1.refs_1_ = bf16[2048,128]{1,0:T(8,128)(2,1)S(1)} collective-permute-done((bf16[2048,128]{1,0:T(8,128)(2,1)S(1)}, bf16[2048,128]{1,0:T(8,128)(2,1)S(1)}, u32[]{:S(2)}, u32[]{:S(2)}) %collective-permute-start.1) | collective-permute-done | bytes 524320 | tf_op jit(solution)/shard_map/ppermute | solution.py:47
  19.3 0.1 collective-permute-start.3
  19.4 2.7 %collective-permute-start.19 = (bf16[128,512]{1,0:T(8,128)(2,1)}, bf16[128,512]{1,0:T(8,128)(2,1)S(1)}, u32[]{:S(2)}, u32[]{:S(2)}) collective-permute-start(bf16[128,512]{1,0:T(8,128)(2,1)} %get-tuple-element.14), channel_id=1, source_target_pairs={{0,128},{16,144},{64,192},{80,208},{128,0},{144,16},{192,64},{208,... | collective-permute-start | bytes 393224 | tf_op jit(solution)/shard_map/ppermute | solution.py:42
  22.1 1.9 %collective-permute-start.2 = (bf16[2048,128]{1,0:T(8,128)(2,1)S(1)}, bf16[2048,128]{1,0:T(8,128)(2,1)S(1)}, u32[]{:S(2)}, u32[]{:S(2)}) collective-permute-start(bf16[2048,128]{1,0:T(8,128)(2,1)S(1)} %collective-permute-done.1.refs_1_), channel_id=1, source_target_pairs={{0,16},{16,0},{1,17},{17,1},{2,18},{18,2},{3,19},{19,3},{4,20},{20... | collective-permute-start | bytes 1572872 | tf_op jit(solution)/shard_map/ppermute | solution.py:30
  23.9 1.5 %shard_map.46.table = s32[48]{0:T(128)} custom-call(s32[16]{0:T(128)} %contract.1, s32[16]{0:T(128)} %column.1), custom_call_target="tpu_custom_call" | custom-call | tf_op jit(solution)/shard_map/pallas_call | solution.py:106
  25.4 0.0 collective-permute-done.19.across
  25.4 0.0 copy-start.2
  25.4 0.6 copy-done.3
  26.0 0.1 copy-done.2
  26.1 1.9 %shard_map.48 = (bf16[256,256]{1,0:T(8,128)(2,1)}, bf16[256,256]{1,0:T(8,128)(2,1)}) custom-call(s32[48]{0:T(128)} %shard_map.46.table, bf16[128,512]{1,0:T(8,128)(2,1)} %get-tuple-element.11.own, bf16[256,512]{1,0:T(8,128)(2,1)} %copy-done.2, bf16[128,512]{1,0:T(8,128)(2,1)} %copy-done.3), custom_call_target="tpu_custom_call" | custom-call | tf_op jit(solution)/shard_map/pallas_call | solution.py:164
  28.0 2.2 %collective-permute-start.20 = (bf16[256,256]{1,0:T(8,128)(2,1)}, bf16[256,256]{1,0:T(8,128)(2,1)S(1)}, u32[]{:S(2)}, u32[]{:S(2)}) collective-permute-start(bf16[256,256]{1,0:T(8,128)(2,1)} %get-tuple-element.16), channel_id=1, source_target_pairs={{0,16},{16,0},{1,17},{17,1},{2,18},{18,2},{3,19},{19,3},{4,20},{20... | collective-permute-start | bytes 393224 | tf_op jit(solution)/shard_map/ppermute | solution.py:30
  30.2 0.1 collective-permute-start.11
  30.3 2.7 %collective-permute-start.4 = (bf16[2048,128]{1,0:T(8,128)(2,1)S(1)}, bf16[2048,128]{1,0:T(8,128)(2,1)S(1)}, u32[]{:S(2)}, u32[]{:S(2)}) collective-permute-start(bf16[2048,128]{1,0:T(8,128)(2,1)S(1)} %constant_dynamic-update-slice_fusion), channel_id=1, source_target_pairs={{0,4},{16,28},{4,8},{20,16},{8,12},{24,20},{12,0},{28,24},{1,5},{1... | collective-permute-start | bytes 1572872 | tf_op jit(solution)/shard_map/ppermute | solution.py:37
  33.0 0.0 collective-permute-done.20
  33.0 0.9 add.6
  34.0 5.5 %collective-permute-start.21 = (bf16[256,256]{1,0:T(8,128)(2,1)S(1)}, bf16[256,256]{1,0:T(8,128)(2,1)S(1)}, u32[]{:S(2)}, u32[]{:S(2)}) collective-permute-start(bf16[256,256]{1,0:T(8,128)(2,1)S(1)} %add.6), channel_id=1, source_target_pairs={{0,32},{32,0},{1,33},{33,1},{2,34},{34,2},{3,35},{35,3},{4,36},{36... | collective-permute-start | bytes 393224 | tf_op jit(solution)/shard_map/ppermute | solution.py:179
  39.4 3.6 %collective-permute-done.21 = bf16[256,256]{1,0:T(8,128)(2,1)S(1)} collective-permute-done((bf16[256,256]{1,0:T(8,128)(2,1)S(1)}, bf16[256,256]{1,0:T(8,128)(2,1)S(1)}, u32[]{:S(2)}, u32[]{:S(2)}) %collective-permute-start.21) | collective-permute-done | bytes 131104 | tf_op jit(solution)/shard_map/ppermute | solution.py:179
  43.0 2.8 %collective-permute-start.25 = (bf16[256,256]{1,0:T(8,128)(2,1)S(1)}, bf16[256,256]{1,0:T(8,128)(2,1)S(1)}, u32[]{:S(2)}, u32[]{:S(2)}) collective-permute-start(bf16[256,256]{1,0:T(8,128)(2,1)S(1)} %add.7), channel_id=1, source_target_pairs={{0,128},{16,144},{64,192},{80,208},{128,0},{144,16},{192,64},{208,... | collective-permute-start | bytes 393224 | tf_op jit(solution)/shard_map/ppermute | solution.py:42
  45.9 0.7 collective-permute-start.22
  46.5 1.7 %collective-permute-start.7 = (bf16[2048,128]{1,0:T(8,128)(2,1)S(1)}, bf16[2048,128]{1,0:T(8,128)(2,1)S(1)}, u32[]{:S(2)}, u32[]{:S(2)}) collective-permute-start(bf16[2048,128]{1,0:T(8,128)(2,1)S(1)} %collective-permute-done.1.refs_1_), channel_id=1, source_target_pairs={{0,4},{16,28},{4,8},{20,16},{8,12},{24,20},{12,0},{28,24},{1,5},{1... | collective-permute-start | bytes 1572872 | tf_op jit(solution)/shard_map/ppermute | solution.py:37
  48.3 0.9 collective-permute-start.12
  49.2 0.5 collective-permute-start.9
  49.7 0.9 collective-permute-start.23
  50.7 0.6 collective-permute-start.6
  51.3 5.2 %collective-permute-done.23.refs_17_ = bf16[512,256]{1,0:T(8,128)(2,1)S(1)} collective-permute-done((bf16[512,256]{1,0:T(8,128)(2,1)S(1)}, bf16[512,256]{1,0:T(8,128)(2,1)S(1)}, u32[]{:S(2)}, u32[]{:S(2)}) %collective-permute-start.23) | collective-permute-done | bytes 262176 | tf_op jit(solution)/shard_map/ppermute | solution.py:42
  56.5 0.0 collective-permute-start.5
  56.6 12.4 %collective-permute-done.6.refs_6_ = bf16[1024,128]{1,0:T(8,128)(2,1)S(1)} collective-permute-done((bf16[1024,128]{1,0:T(8,128)(2,1)S(1)}, bf16[1024,128]{1,0:T(8,128)(2,1)S(1)}, u32[]{:S(2)}, u32[]{:S(2)}) %collective-permute-start.6) | collective-permute-done | bytes 262176 | tf_op jit(solution)/shard_map/ppermute | solution.py:37
  68.9 2.1 %collective-permute-start.24 = (bf16[512,256]{1,0:T(8,128)(2,1)S(1)}, bf16[512,256]{1,0:T(8,128)(2,1)S(1)}, u32[]{:S(2)}, u32[]{:S(2)}) collective-permute-start(bf16[512,256]{1,0:T(8,128)(2,1)S(1)} %collective-permute-done.23.refs_17_), channel_id=1, source_target_pairs={{0,16},{16,0},{1,17},{17,1},{2,18},{18,2},{3,19},{19,3},{4,20},{20... | collective-permute-start | bytes 786440 | tf_op jit(solution)/shard_map/ppermute | solution.py:30
  71.0 4.0 %collective-permute-start.15 = (bf16[1024,128]{1,0:T(8,128)(2,1)S(1)}, bf16[1024,128]{1,0:T(8,128)(2,1)S(1)}, u32[]{:S(2)}, u32[]{:S(2)}) collective-permute-start(bf16[1024,128]{1,0:T(8,128)(2,1)S(1)} %collective-permute-done.6.refs_6_), channel_id=1, source_target_pairs={{0,2},{16,18},{1,3},{17,19},{2,0},{18,16},{3,1},{19,17},{4,6},{20,... | collective-permute-start | bytes 786440 | tf_op jit(solution)/shard_map/ppermute | solution.py:47
  75.0 0.4 collective-permute-start.26
  75.4 0.8 collective-permute-start.14
  76.2 0.2 collective-permute-done.26.refs_20_
  76.4 0.6 collective-permute-start.8
  77.1 1.1 %collective-permute-start.16 = (bf16[1024,128]{1,0:T(8,128)(2,1)S(1)}, bf16[1024,128]{1,0:T(8,128)(2,1)S(1)}, u32[]{:S(2)}, u32[]{:S(2)}) collective-permute-start(bf16[1024,128]{1,0:T(8,128)(2,1)S(1)} %get-tuple-element.17), channel_id=1, source_target_pairs={{0,4},{16,28},{4,8},{20,16},{8,12},{24,20},{12,0},{28,24},{1,5},{1... | collective-permute-start | bytes 786440 | tf_op jit(solution)/shard_map/ppermute | solution.py:37
  78.2 9.1 %collective-permute-done.15.refs_14_ = bf16[1024,128]{1,0:T(8,128)(2,1)S(1)} collective-permute-done((bf16[1024,128]{1,0:T(8,128)(2,1)S(1)}, bf16[1024,128]{1,0:T(8,128)(2,1)S(1)}, u32[]{:S(2)}, u32[]{:S(2)}) %collective-permute-start.15) | collective-permute-done | bytes 262176 | tf_op jit(solution)/shard_map/ppermute | solution.py:47
  87.3 0.6 collective-permute-start.10
  87.9 1.1 %collective-permute-done.10.refs_10_ = bf16[1024,128]{1,0:T(8,128)(2,1)S(1)} collective-permute-done((bf16[1024,128]{1,0:T(8,128)(2,1)S(1)}, bf16[1024,128]{1,0:T(8,128)(2,1)S(1)}, u32[]{:S(2)}, u32[]{:S(2)}) %collective-permute-start.10) | collective-permute-done | bytes 262176 | tf_op jit(solution)/shard_map/ppermute | solution.py:30
  89.0 0.7 copy-done.1
  89.7 6.2 %shard_map.49 = f32[1024,2048]{1,0:T(8,128)} custom-call(s32[48]{0:T(128)S(1)} %copy-done.1, bf16[1024,128]{1,0:T(8,128)(2,1)S(1)} %copy-done, bf16[2048,128]{1,0:T(8,128)(2,1)S(1)} %collective-permute-done.1.refs_1_, bf16[2048,128]{1,0:T(8,128)(2,1)S(1)} %collective-permute-done.2.refs_2_, bf16[1024,128]{1,0:T(8,128)(2,1)S(1)} %collective-permute-done.3.refs_3_, ...), custom_call_target="tpu_custom_call" | custom-call | flops 1073741824 | bytes 8388608 | tf_op jit(solution)/shard_map/pallas_call | solution.py:253
  (30 shorter events, 0.3 us)
Async XLA Ops:
  0.0 89.0 %copy-start = (bf16[1024,128]{1,0:T(8,128)(2,1)S(1)}, bf16[1024,128]{1,0:T(8,128)(2,1)}, u32[]{:S(2)}) copy-start(bf16[1024,128]{1,0:T(8,128)(2,1)} %refs_0_.1) | copy-start | bytes 786436
  0.0 4.6 %collective-permute-start = (bf16[1024,128]{1,0:T(8,128)(2,1)}, bf16[1024,128]{1,0:T(8,128)(2,1)S(1)}, u32[]{:S(2)}, u32[]{:S(2)}) collective-permute-start(bf16[1024,128]{1,0:T(8,128)(2,1)} %refs_0_.1), channel_id=1, source_target_pairs={{0,16},{16,0},{1,17},{17,1},{2,18},{18,2},{3,19},{19,3},{4,20},{20... | collective-permute-start | bytes 786440 | tf_op jit(solution)/shard_map/ppermute | solution.py:30
  4.7 14.6 %collective-permute-start.1 = (bf16[2048,128]{1,0:T(8,128)(2,1)S(1)}, bf16[2048,128]{1,0:T(8,128)(2,1)S(1)}, u32[]{:S(2)}, u32[]{:S(2)}) collective-permute-start(bf16[2048,128]{1,0:T(8,128)(2,1)S(1)} %constant_dynamic-update-slice_fusion), channel_id=1, source_target_pairs={{0,1},{16,18},{1,0},{17,19},{2,3},{18,16},{3,2},{19,17},{4,5},{20,... | collective-permute-start | bytes 1572872 | tf_op jit(solution)/shard_map/ppermute | solution.py:47
  7.9 1.6 %collective-permute-start.17 = (bf16[128,512]{1,0:T(8,128)(2,1)}, bf16[128,512]{1,0:T(8,128)(2,1)S(1)}, u32[]{:S(2)}, u32[]{:S(2)}) collective-permute-start(bf16[128,512]{1,0:T(8,128)(2,1)} %get-tuple-element.13), channel_id=1, source_target_pairs={{0,16},{16,0},{1,17},{17,1},{2,18},{18,2},{3,19},{19,3},{4,20},{20... | collective-permute-start | bytes 393224 | tf_op jit(solution)/shard_map/ppermute | solution.py:30
  10.5 14.9 %collective-permute-start.18 = (bf16[256,512]{1,0:T(8,128)(2,1)S(1)}, bf16[256,512]{1,0:T(8,128)(2,1)S(1)}, u32[]{:S(2)}, u32[]{:S(2)}) collective-permute-start(bf16[256,512]{1,0:T(8,128)(2,1)S(1)} %pad_maximum_fusion.1), channel_id=1, source_target_pairs={{0,64},{16,208},{64,0},{80,144},{128,192},{144,80},{192,128},{208,... | collective-permute-start | bytes 786440 | tf_op jit(solution)/shard_map/ppermute | solution.py:42
  19.3 10.9 %collective-permute-start.3 = (bf16[1024,128]{1,0:T(8,128)(2,1)S(1)}, bf16[1024,128]{1,0:T(8,128)(2,1)S(1)}, u32[]{:S(2)}, u32[]{:S(2)}) collective-permute-start(bf16[1024,128]{1,0:T(8,128)(2,1)S(1)} %slice.28), channel_id=1, source_target_pairs={{0,2},{16,17},{1,3},{17,16},{2,0},{18,19},{3,1},{19,18},{4,6},{20,... | collective-permute-start | bytes 786440 | tf_op jit(solution)/shard_map/ppermute | solution.py:47
  19.4 6.0 %collective-permute-start.19 = (bf16[128,512]{1,0:T(8,128)(2,1)}, bf16[128,512]{1,0:T(8,128)(2,1)S(1)}, u32[]{:S(2)}, u32[]{:S(2)}) collective-permute-start(bf16[128,512]{1,0:T(8,128)(2,1)} %get-tuple-element.14), channel_id=1, source_target_pairs={{0,128},{16,144},{64,192},{80,208},{128,0},{144,16},{192,64},{208,... | collective-permute-start | bytes 393224 | tf_op jit(solution)/shard_map/ppermute | solution.py:42
  22.1 27.1 %collective-permute-start.2 = (bf16[2048,128]{1,0:T(8,128)(2,1)S(1)}, bf16[2048,128]{1,0:T(8,128)(2,1)S(1)}, u32[]{:S(2)}, u32[]{:S(2)}) collective-permute-start(bf16[2048,128]{1,0:T(8,128)(2,1)S(1)} %collective-permute-done.1.refs_1_), channel_id=1, source_target_pairs={{0,16},{16,0},{1,17},{17,1},{2,18},{18,2},{3,19},{19,3},{4,20},{20... | collective-permute-start | bytes 1572872 | tf_op jit(solution)/shard_map/ppermute | solution.py:30
  25.4 0.6 copy-start.3
  25.4 0.7 copy-start.2
  28.0 5.0 %collective-permute-start.20 = (bf16[256,256]{1,0:T(8,128)(2,1)}, bf16[256,256]{1,0:T(8,128)(2,1)S(1)}, u32[]{:S(2)}, u32[]{:S(2)}) collective-permute-start(bf16[256,256]{1,0:T(8,128)(2,1)} %get-tuple-element.16), channel_id=1, source_target_pairs={{0,16},{16,0},{1,17},{17,1},{2,18},{18,2},{3,19},{19,3},{4,20},{20... | collective-permute-start | bytes 393224 | tf_op jit(solution)/shard_map/ppermute | solution.py:30
  30.2 16.4 %collective-permute-start.11 = (bf16[1024,128]{1,0:T(8,128)(2,1)S(1)}, bf16[1024,128]{1,0:T(8,128)(2,1)S(1)}, u32[]{:S(2)}, u32[]{:S(2)}) collective-permute-start(bf16[1024,128]{1,0:T(8,128)(2,1)S(1)} %collective-permute-done.3.refs_3_), channel_id=1, source_target_pairs={{0,16},{16,0},{1,17},{17,1},{2,18},{18,2},{3,19},{19,3},{4,20},{20... | collective-permute-start | bytes 786440 | tf_op jit(solution)/shard_map/ppermute | solution.py:30
  30.3 19.4 %collective-permute-start.4 = (bf16[2048,128]{1,0:T(8,128)(2,1)S(1)}, bf16[2048,128]{1,0:T(8,128)(2,1)S(1)}, u32[]{:S(2)}, u32[]{:S(2)}) collective-permute-start(bf16[2048,128]{1,0:T(8,128)(2,1)S(1)} %constant_dynamic-update-slice_fusion), channel_id=1, source_target_pairs={{0,4},{16,28},{4,8},{20,16},{8,12},{24,20},{12,0},{28,24},{1,5},{1... | collective-permute-start | bytes 1572872 | tf_op jit(solution)/shard_map/ppermute | solution.py:37
  34.0 9.0 %collective-permute-start.21 = (bf16[256,256]{1,0:T(8,128)(2,1)S(1)}, bf16[256,256]{1,0:T(8,128)(2,1)S(1)}, u32[]{:S(2)}, u32[]{:S(2)}) collective-permute-start(bf16[256,256]{1,0:T(8,128)(2,1)S(1)} %add.6), channel_id=1, source_target_pairs={{0,32},{32,0},{1,33},{33,1},{2,34},{34,2},{3,35},{35,3},{4,36},{36... | collective-permute-start | bytes 393224 | tf_op jit(solution)/shard_map/ppermute | solution.py:179
  43.0 7.7 %collective-permute-start.25 = (bf16[256,256]{1,0:T(8,128)(2,1)S(1)}, bf16[256,256]{1,0:T(8,128)(2,1)S(1)}, u32[]{:S(2)}, u32[]{:S(2)}) collective-permute-start(bf16[256,256]{1,0:T(8,128)(2,1)S(1)} %add.7), channel_id=1, source_target_pairs={{0,128},{16,144},{64,192},{80,208},{128,0},{144,16},{192,64},{208,... | collective-permute-start | bytes 393224 | tf_op jit(solution)/shard_map/ppermute | solution.py:42
  45.9 2.4 %collective-permute-start.22 = (bf16[256,256]{1,0:T(8,128)(2,1)S(1)}, bf16[256,256]{1,0:T(8,128)(2,1)S(1)}, u32[]{:S(2)}, u32[]{:S(2)}) collective-permute-start(bf16[256,256]{1,0:T(8,128)(2,1)S(1)} %add.7), channel_id=1, source_target_pairs={{0,16},{16,0},{1,17},{17,1},{2,18},{18,2},{3,19},{19,3},{4,20},{20... | collective-permute-start | bytes 393224 | tf_op jit(solution)/shard_map/ppermute | solution.py:30
  46.5 24.4 %collective-permute-start.7 = (bf16[2048,128]{1,0:T(8,128)(2,1)S(1)}, bf16[2048,128]{1,0:T(8,128)(2,1)S(1)}, u32[]{:S(2)}, u32[]{:S(2)}) collective-permute-start(bf16[2048,128]{1,0:T(8,128)(2,1)S(1)} %collective-permute-done.1.refs_1_), channel_id=1, source_target_pairs={{0,4},{16,28},{4,8},{20,16},{8,12},{24,20},{12,0},{28,24},{1,5},{1... | collective-permute-start | bytes 1572872 | tf_op jit(solution)/shard_map/ppermute | solution.py:37
  48.3 27.1 %collective-permute-start.12 = (bf16[2048,128]{1,0:T(8,128)(2,1)S(1)}, bf16[2048,128]{1,0:T(8,128)(2,1)S(1)}, u32[]{:S(2)}, u32[]{:S(2)}) collective-permute-start(bf16[2048,128]{1,0:T(8,128)(2,1)S(1)} %pad_maximum_fusion), channel_id=1, source_target_pairs={{0,4},{16,28},{4,8},{20,16},{8,12},{24,20},{12,0},{28,24},{1,5},{1... | collective-permute-start | bytes 1572872 | tf_op jit(solution)/shard_map/ppermute | solution.py:37
  49.2 25.8 %collective-permute-start.9 = (bf16[2048,128]{1,0:T(8,128)(2,1)S(1)}, bf16[2048,128]{1,0:T(8,128)(2,1)S(1)}, u32[]{:S(2)}, u32[]{:S(2)}) collective-permute-start(bf16[2048,128]{1,0:T(8,128)(2,1)S(1)} %collective-permute-done.2.refs_2_), channel_id=1, source_target_pairs={{0,4},{16,28},{4,8},{20,16},{8,12},{24,20},{12,0},{28,24},{1,5},{1... | collective-permute-start | bytes 1572872 | tf_op jit(solution)/shard_map/ppermute | solution.py:37
  49.7 6.8 %collective-permute-start.23 = (bf16[512,256]{1,0:T(8,128)(2,1)S(1)}, bf16[512,256]{1,0:T(8,128)(2,1)S(1)}, u32[]{:S(2)}, u32[]{:S(2)}) collective-permute-start(bf16[512,256]{1,0:T(8,128)(2,1)S(1)} %pad_maximum_fusion.2.refs_16_), channel_id=1, source_target_pairs={{0,64},{16,208},{64,0},{80,144},{128,192},{144,80},{192,128},{208,... | collective-permute-start | bytes 786440 | tf_op jit(solution)/shard_map/ppermute | solution.py:42
  50.7 18.2 %collective-permute-start.6 = (bf16[1024,128]{1,0:T(8,128)(2,1)S(1)}, bf16[1024,128]{1,0:T(8,128)(2,1)S(1)}, u32[]{:S(2)}, u32[]{:S(2)}) collective-permute-start(bf16[1024,128]{1,0:T(8,128)(2,1)S(1)} %get-tuple-element.19), channel_id=1, source_target_pairs={{0,4},{16,28},{4,8},{20,16},{8,12},{24,20},{12,0},{28,24},{1,5},{1... | collective-permute-start | bytes 786440 | tf_op jit(solution)/shard_map/ppermute | solution.py:37
  56.5 20.6 %collective-permute-start.5 = (bf16[1024,128]{1,0:T(8,128)(2,1)S(1)}, bf16[1024,128]{1,0:T(8,128)(2,1)S(1)}, u32[]{:S(2)}, u32[]{:S(2)}) collective-permute-start(bf16[1024,128]{1,0:T(8,128)(2,1)S(1)} %get-tuple-element.20), channel_id=1, source_target_pairs={{0,16},{16,0},{1,17},{17,1},{2,18},{18,2},{3,19},{19,3},{4,20},{20... | collective-permute-start | bytes 786440 | tf_op jit(solution)/shard_map/ppermute | solution.py:30
  68.9 9.3 %collective-permute-start.24 = (bf16[512,256]{1,0:T(8,128)(2,1)S(1)}, bf16[512,256]{1,0:T(8,128)(2,1)S(1)}, u32[]{:S(2)}, u32[]{:S(2)}) collective-permute-start(bf16[512,256]{1,0:T(8,128)(2,1)S(1)} %collective-permute-done.23.refs_17_), channel_id=1, source_target_pairs={{0,16},{16,0},{1,17},{17,1},{2,18},{18,2},{3,19},{19,3},{4,20},{20... | collective-permute-start | bytes 786440 | tf_op jit(solution)/shard_map/ppermute | solution.py:30
  71.0 16.3 %collective-permute-start.15 = (bf16[1024,128]{1,0:T(8,128)(2,1)S(1)}, bf16[1024,128]{1,0:T(8,128)(2,1)S(1)}, u32[]{:S(2)}, u32[]{:S(2)}) collective-permute-start(bf16[1024,128]{1,0:T(8,128)(2,1)S(1)} %collective-permute-done.6.refs_6_), channel_id=1, source_target_pairs={{0,2},{16,18},{1,3},{17,19},{2,0},{18,16},{3,1},{19,17},{4,6},{20,... | collective-permute-start | bytes 786440 | tf_op jit(solution)/shard_map/ppermute | solution.py:47
  75.0 1.4 %collective-permute-start.26 = (bf16[256,256]{1,0:T(8,128)(2,1)S(1)}, bf16[256,256]{1,0:T(8,128)(2,1)S(1)}, u32[]{:S(2)}, u32[]{:S(2)}) collective-permute-start(bf16[256,256]{1,0:T(8,128)(2,1)S(1)} %collective-permute-done.25.refs_19_), channel_id=1, source_target_pairs={{0,16},{16,0},{1,17},{17,1},{2,18},{18,2},{3,19},{19,3},{4,20},{20... | collective-permute-start | bytes 393224 | tf_op jit(solution)/shard_map/ppermute | solution.py:30
  75.4 12.4 %collective-permute-start.14 = (bf16[1024,128]{1,0:T(8,128)(2,1)S(1)}, bf16[1024,128]{1,0:T(8,128)(2,1)S(1)}, u32[]{:S(2)}, u32[]{:S(2)}) collective-permute-start(bf16[1024,128]{1,0:T(8,128)(2,1)S(1)} %collective-permute-done.6.refs_6_), channel_id=1, source_target_pairs={{0,1},{16,17},{1,0},{17,16},{2,3},{18,19},{3,2},{19,18},{4,5},{20,... | collective-permute-start | bytes 786440 | tf_op jit(solution)/shard_map/ppermute | solution.py:47
  76.4 11.4 %collective-permute-start.8 = (bf16[1024,128]{1,0:T(8,128)(2,1)S(1)}, bf16[1024,128]{1,0:T(8,128)(2,1)S(1)}, u32[]{:S(2)}, u32[]{:S(2)}) collective-permute-start(bf16[1024,128]{1,0:T(8,128)(2,1)S(1)} %slice.31), channel_id=1, source_target_pairs={{0,16},{16,0},{1,17},{17,1},{2,18},{18,2},{3,19},{19,3},{4,20},{20... | collective-permute-start | bytes 786440 | tf_op jit(solution)/shard_map/ppermute | solution.py:30
  77.1 10.8 %collective-permute-start.16 = (bf16[1024,128]{1,0:T(8,128)(2,1)S(1)}, bf16[1024,128]{1,0:T(8,128)(2,1)S(1)}, u32[]{:S(2)}, u32[]{:S(2)}) collective-permute-start(bf16[1024,128]{1,0:T(8,128)(2,1)S(1)} %get-tuple-element.17), channel_id=1, source_target_pairs={{0,4},{16,28},{4,8},{20,16},{8,12},{24,20},{12,0},{28,24},{1,5},{1... | collective-permute-start | bytes 786440 | tf_op jit(solution)/shard_map/ppermute | solution.py:37
  78.2 9.7 %collective-permute-start.13 = (bf16[1024,128]{1,0:T(8,128)(2,1)S(1)}, bf16[1024,128]{1,0:T(8,128)(2,1)S(1)}, u32[]{:S(2)}, u32[]{:S(2)}) collective-permute-start(bf16[1024,128]{1,0:T(8,128)(2,1)S(1)} %get-tuple-element.18), channel_id=1, source_target_pairs={{0,16},{16,0},{1,17},{17,1},{2,18},{18,2},{3,19},{19,3},{4,20},{20... | collective-permute-start | bytes 786440 | tf_op jit(solution)/shard_map/ppermute | solution.py:30
  87.3 1.7 %collective-permute-start.10 = (bf16[1024,128]{1,0:T(8,128)(2,1)S(1)}, bf16[1024,128]{1,0:T(8,128)(2,1)S(1)}, u32[]{:S(2)}, u32[]{:S(2)}) collective-permute-start(bf16[1024,128]{1,0:T(8,128)(2,1)S(1)} %slice.32), channel_id=1, source_target_pairs={{0,16},{16,0},{1,17},{17,1},{2,18},{18,2},{3,19},{19,3},{4,20},{20... | collective-permute-start | bytes 786440 | tf_op jit(solution)/shard_map/ppermute | solution.py:30
  89.0 0.7 copy-start.1

commit v3 on v2

v3 whole, which is shorter than its diff:
```python
import functools

import jax
import jax.numpy as jnp
from jax import lax
from jax.experimental import pallas as pl
from jax.experimental.pallas import tpu as pltpu
from jax.sharding import Mesh, PartitionSpec as P

P_SIZE = 128
SYMS = 8
OCC = ("x", "zh", "core")
VIR = ("y", "zl")
NX = NY = NZ = 4
NK = 16
QUARTER = 4
STEP = 256

SLOTS = 0
MERGE = 2 * NK
HALVES = MERGE + 2 * QUARTER
TABLE = HALVES + 2 * QUARTER

VMEM = pl.BlockSpec(memory_space=pltpu.VMEM)
SMEM = pl.BlockSpec(memory_space=pltpu.SMEM)
ANY = pl.BlockSpec(memory_space=pl.ANY)


def send(name, value, axes, pairs, *others):
    with jax.named_scope(name):
        if others:
            value = lax.optimization_barrier((value, *others))[0]
        return lax.ppermute(value, axes, pairs)


def swap(name, value, *others):
    return send(name, value, "core", [(0, 1), (1, 0)], *others)


def ring(name, value, *others):
    pairs = []
    for y in range(NY):
        pairs += [(y, (y + 1) % NY), (NY + y, NY + (y - 1) % NY)]
    return send(name, value, ("core", "y"), pairs, *others)


def cross_x(name, value, bits, *others):
    pairs = [(2 * x + c, 2 * (x ^ bits[c]) + c) for x in range(NX) for c in range(2)]
    return send(name, value, ("x", "core"), pairs, *others)


def after(value, *others):
    return lax.optimization_barrier((value, *others))[0]


def cross_z(name, value, bits, *others):
    pairs = [(NZ * c + z, NZ * c + (z ^ bits[c])) for z in range(NZ) for c in range(2)]
    return send(name, value, ("core", "zl"), pairs, *others)


def table_kernel(contract, column, out, inverse, rank, chosen):
    x, zh, c = (lax.axis_index(axis) for axis in OCC)
    y, z = (lax.axis_index(axis) for axis in VIR)
    one, two = (y + 3 + 2 * c) % NY, (y + 1 + 2 * c) % NY
    far = (y + 2) % NY
    sources = [(y, z), (y, z ^ 1), (y, z ^ 2), (y, z ^ 3)]
    for bit in range(NZ):
        sources += [(one, z ^ bit), (two, z ^ bit), (far, z ^ bit)]
    for i, (row, col) in enumerate(sources):
        inverse[row * NZ + col] = i
    for s in range(SYMS):
        chosen[2 * SYMS + s] = 0
    for k in range(NK):
        label = contract[k]
        place = chosen[2 * SYMS + label]
        rank[k] = place
        chosen[2 * label + place] = inverse[k]
        chosen[2 * SYMS + label] = place + 1
    for l in range(NK):
        for r in range(2):
            out[SLOTS + r * NK + l] = chosen[2 * column[l] + r]

    near_x, far_x = x ^ (1 + 2 * c), x ^ (3 - 2 * c)
    tiles = [
        x * 4 + zh * 2 + c,
        near_x * 4 + zh * 2 + c,
        near_x * 4 + zh * 2 + 1 - c,
        (x ^ 2) * 4 + zh * 2 + c,
    ]
    for j in range(QUARTER):
        half = c if j < 2 else 1 - c
        label = column[QUARTER * x + 2 * half + j % 2]
        for r in range(2):
            found = jnp.int32(len(tiles))
            for s, tile in enumerate(tiles):
                hit = (contract[tile] == label) & (rank[tile] == r)
                found = jnp.where(hit, s, found)
            out[MERGE + r * QUARTER + j] = found

    halves = [
        (x, c), (x, 1 - c),
        (near_x, c), (near_x, 1 - c),
        (x ^ 2, c),
        (far_x, 1 - c), (far_x, c),
        (x ^ 2, 1 - c),
    ]
    for i, (quarter, half) in enumerate(halves):
        out[HALVES + 2 * quarter + half] = i


def make_table(contract_class, column_class):
    return pl.pallas_call(
        table_kernel,
        out_shape=jax.ShapeDtypeStruct((TABLE,), jnp.int32),
        in_specs=[SMEM, SMEM],
        out_specs=SMEM,
        scratch_shapes=[
            pltpu.SMEM((NK,), jnp.int32),
            pltpu.SMEM((NK,), jnp.int32),
            pltpu.SMEM((3 * SYMS,), jnp.int32),
        ],
    )(contract_class, column_class)


def cut_kernel(integrals, *refs):
    outs, sems = refs[:NX], refs[NX]
    x, c = lax.axis_index("x"), lax.axis_index("core")
    half = outs[0].shape[1] // 2
    quarters = [(x, c), (x ^ (1 + 2 * c), c), (x ^ (3 - 2 * c), 1 - c), (x ^ 2, c)]
    copies = []
    for out, (quarter, first) in zip(outs, quarters):
        for i, side in enumerate((first, 1 - first)):
            start = pl.multiple_of((2 * quarter + side) * half, half)
            source = integrals.at[:, pl.ds(start, half)]
            target = out.at[:, pl.ds(i * half, half)]
            sem = sems.at[len(copies)]
            copies.append(pltpu.make_async_copy(source, target, sem))
    for copy in copies:
        copy.start()
    for copy in copies:
        copy.wait()


def cut(integrals):
    depth, width = integrals.shape
    shape = jax.ShapeDtypeStruct((depth, width // NX), integrals.dtype)
    return pl.pallas_call(
        cut_kernel,
        out_shape=[shape] * NX,
        in_specs=[ANY],
        out_specs=[VMEM] * NX,
        scratch_shapes=[pltpu.SemaphoreType.DMA((2 * NX,))],
    )(integrals)


def merge(table, tiles):
    found = table[MERGE : MERGE + 2 * QUARTER].reshape(2, 1, QUARTER)
    found = jnp.repeat(found, P_SIZE, axis=2)
    total = jnp.zeros_like(tiles[0])[None]
    for s, tile in enumerate(tiles):
        total = jnp.where(found == s, tile[None], total)
    return total.reshape(2 * P_SIZE, -1)


def exchange(amplitudes, integrals, contract_class, column_class):
    rows = amplitudes.shape[0]

    def doubled(name, value, *others):
        return jnp.concatenate([value, swap(name, value, *others)])

    own = amplitudes
    z2 = cross_z("z2", own, (2, 2))
    z1 = cross_z("z1", own, (1, 1))
    pair0 = doubled("swap0", own)
    up0 = ring("up0", pair0)
    quarter, near, far, across = cut(integrals)
    near = jnp.concatenate([near, swap("r0", far)])
    near = cross_x("r1", near, (1, 3))
    across = cross_x("r2", across, (2, 2))
    table = make_table(contract_class, column_class)
    far0 = ring("far0", up0[:rows])

    line = jnp.concatenate([z1, z2])
    turned = swap("turned", line)
    up12 = ring("up12", jnp.concatenate([line, turned]))
    z3 = cross_z("z3", z2, (1, 1))
    tiles = [quarter, near[:P_SIZE], near[P_SIZE:], across]
    merged = merge(table, tiles)
    width = merged.shape[1] // 2
    part = merged[:, :width] + swap("c1", merged[:, width:])

    pair3 = doubled("swap3", z3, turned)
    up3 = ring("up3", pair3, up12)
    moved = send("zh", part, "zh", [(0, 1), (1, 0)], turned)
    part = part + moved
    far1 = cross_z("far1", far0, (1, 1))
    far2 = ring("far2", up12[rows : 2 * rows])

    pair = doubled("c2", part)
    near = cross_x("g1", pair, (1, 3), moved)
    across = cross_x("g2", part, (2, 2))
    down = jnp.concatenate([up0[rows:], up12[2 * rows :]])
    down = swap("down", down)
    far3 = ring("far3", up3[:rows], far2)
    down3 = swap("down3", up3[rows:])
    both = jnp.concatenate([near, across])
    both_swapped = swap("c34", both)
    parts = [pair, both, both_swapped]
    pieces = [(own, 0), (line, 0), (line, rows), (z3, 0)]
    pieces += [(up0, 0), (down, 0), (far0, 0)]
    pieces += [(up12, 0), (down, rows), (far1, 0)]
    pieces += [(up12, rows), (down, 2 * rows), (far2, 0)]
    pieces += [(up3, 0), (down3, 0), (far3, 0)]
    return table, pieces, parts


def multiply_kernel(spots, table, *refs):
    count = len(refs) - 4
    pieces, parts = refs[: count - 3], refs[count - 3 : count]
    out, amps, slab, sems = refs[count:]
    rows = amps.shape[1]

    @pl.when(pl.program_id(0) == 0)
    def _():
        copies = []
        for i, (which, start) in enumerate(spots):
            source = pieces[which].at[pl.ds(start, rows)]
            copies.append(pltpu.make_async_copy(source, amps.at[i], sems.at[i]))
        place = 0
        for i, part in enumerate(parts):
            size = part.shape[0]
            target = slab.at[pl.ds(place, size)]
            copies.append(pltpu.make_async_copy(part, target, sems.at[NK + i]))
            place += size
        for copy in copies:
            copy.start()
        for copy in copies:
            copy.wait()

    block = pl.ds(pl.multiple_of(pl.program_id(0) * STEP, STEP), STEP)
    depth = 2 * P_SIZE
    for l in range(NK):
        pair = jnp.concatenate(
            [amps[table[SLOTS + r * NK + l], block] for r in range(2)], axis=1
        )
        place = pl.multiple_of(table[HALVES + l // 2] * depth, depth)
        lane = (l % 2) * P_SIZE
        weights = slab[pl.ds(place, depth), lane : lane + P_SIZE]
        out[:, l * P_SIZE : (l + 1) * P_SIZE] = jnp.dot(
            pair, weights, preferred_element_type=jnp.float32
        )


def multiply(table, pieces, parts):
    rows = pieces[0][0].shape[0]
    arrays, spots = [], []
    for piece, start in pieces:
        if not any(piece is array for array in arrays):
            arrays.append(piece)
        which = [piece is array for array in arrays].index(True)
        spots.append((which, start))
    width = NK * P_SIZE
    return pl.pallas_call(
        functools.partial(multiply_kernel, tuple(spots)),
        out_shape=jax.ShapeDtypeStruct((rows, width), jnp.float32),
        grid_spec=pltpu.PrefetchScalarGridSpec(
            num_scalar_prefetch=1,
            grid=(rows // STEP,),
            in_specs=[ANY] * (len(arrays) + len(parts)),
            out_specs=pl.BlockSpec((STEP, width), lambda i, table: (i, 0)),
            scratch_shapes=[
                pltpu.VMEM((NK, rows, P_SIZE), jnp.bfloat16),
                pltpu.VMEM((2 * NK * P_SIZE // 2, 2 * P_SIZE), jnp.bfloat16),
                pltpu.SemaphoreType.DMA((NK + len(parts),)),
            ],
        ),
        compiler_params=pltpu.CompilerParams(vmem_limit_bytes=24 * 1024 * 1024),
        cost_estimate=pl.CostEstimate(
            flops=4 * rows * P_SIZE * width,
            bytes_accessed=4 * rows * width,
            transcendentals=0,
        ),
    )(table, *arrays, *parts)


def body(amplitudes, integrals, contract_class, column_class):
    table, pieces, parts = exchange(
        amplitudes, integrals, contract_class, column_class
    )
    return multiply(table, pieces, parts)


def solution(mesh):
    fine = Mesh(mesh.devices.reshape(NX, 2, 2, NY, NZ), OCC + VIR)
    placed = (P(OCC, VIR), P(OCC, VIR), P(), P(VIR))
    return jax.shard_map(
        body, mesh=fine, in_specs=placed, out_specs=P(OCC, VIR), check_vma=False
    )
```

time: 96.3 us -> 71.1 us (0.74)
  the two profiles are of different devices: /device:TPU:1 before, /device:TPU:32 now
where the time goes in v3:
time: 71.1 us; the launch traced here: 70.9 us
  waiting for transfers between devices  34.4 us (48%)
  starting transfers between devices  23.6 us (33%)
  Pallas kernels  9.6 us (14%)
  other arithmetic  2 us (3%)
  local copies, waits for them, and re-layouts  0.91 us (1%)
    ppermute x24, waiting for transfers between devices, send(): return lax.ppermute(value, axes, pairs)  34.4 us
    ppermute x24, starting transfers between devices, send(): return lax.ppermute(value, axes, pairs)  23.6 us
    pallas_call x1, Pallas kernels, multiply(): pl.pallas_call(functools.partial(multiply_kernel, tuple(spots)), out_shap...  6.22 us
    pallas_call x1, Pallas kernels, cut(): pl.pallas_call(cut_kernel, out_shape=[shape] * NX, in_specs=[ANY], out_sp...  1.92 us
    pallas_call x1, Pallas kernels, make_table(): pl.pallas_call(table_kernel, out_shape=jax.ShapeDtypeStruct((TABLE,), jnp...  1.45 us
  transfers between devices with their start and end apart: 24, of which 10 were waited for; matrix products, arithmetic and copies ran while one was open for 4% of the time, Pallas kernels for 5%

profile of v3, /device:TPU:32, one launch (start us, length us, event | category | flops | bytes accessed | tf_op | source)
XLA Modules:
  0.0 70.9 jit_solution(14530362457916179272)
XLA Ops:
  0.0 0.0 collective-permute-start.3
  0.0 3.4 %collective-permute-start.1 = (bf16[1024,128]{1,0:T(8,128)(2,1)}, bf16[1024,128]{1,0:T(8,128)(2,1)S(1)}, u32[]{:S(2)}, u32[]{:S(2)}) collective-permute-start(bf16[1024,128]{1,0:T(8,128)(2,1)} %refs_0_.1), channel_id=1, source_target_pairs={{0,2},{16,18},{1,3},{17,19},{2,0},{18,16},{3,1},{19,17},{4,6},{20,... | collective-permute-start | bytes 786440 | tf_op jit(solution)/shard_map/z2/ppermute | solution.py:33
  3.4 0.1 collective-permute-start
  3.5 1.9 %shard_map.47 = (bf16[128,512]{1,0:T(8,128)(2,1)}, bf16[128,512]{1,0:T(8,128)(2,1)}, bf16[128,512]{1,0:T(8,128)(2,1)}, bf16[128,512]{1,0:T(8,128)(2,1)}) custom-call(bf16[128,2048]{1,0:T(8,128)(2,1)} %integrals.1), custom_call_target="tpu_custom_call" | custom-call | tf_op jit(solution)/shard_map/pallas_call | solution.py:147
  5.4 0.0 copy-start.2
  5.4 3.1 %collective-permute-start.15 = (bf16[128,512]{1,0:T(8,128)(2,1)}, bf16[128,512]{1,0:T(8,128)(2,1)S(1)}, u32[]{:S(2)}, u32[]{:S(2)}) collective-permute-start(bf16[128,512]{1,0:T(8,128)(2,1)} %get-tuple-element.17), channel_id=1, source_target_pairs={{0,128},{16,144},{64,192},{80,208},{128,0},{144,16},{192,64},{208,... | collective-permute-start | bytes 393224 | tf_op jit(solution)/shard_map/r2/ppermute | solution.py:33
  8.5 1.5 %shard_map.46.table = s32[48]{0:T(128)} custom-call(s32[16]{0:T(128)} %contract.1, s32[16]{0:T(128)} %column.1), custom_call_target="tpu_custom_call" | custom-call | tf_op jit(solution)/shard_map/pallas_call | solution.py:112
  10.0 0.7 %broadcast_compare_fusion.3 = (pred[8]{0:T(512)(128)(4,1)S(1)}, pred[8]{0:T(512)(128)(4,1)S(1)}, pred[8]{0:T(512)(128)(4,1)S(1)}, pred[8]{0:T(512)(128)(4,1)S(1)}) fusion(s32[48]{0:T(128)} %shard_map.46.table), kind=kLoop, calls=%fused_computation.23 | loop fusion | flops 32 | bytes 64 | tf_op jit(solution)/shard_map/eq | solution.py:161
  10.7 0.1 eq.74
  10.8 0.1 broadcast_bitcast_fusion.3
  10.9 0.1 eq.78
  11.0 0.1 broadcast_bitcast_fusion.2
  11.1 0.1 eq.82
  11.1 0.1 broadcast_bitcast_fusion.1
  11.2 0.1 eq.86
  11.3 0.1 broadcast_bitcast_fusion
  11.4 0.9 %pad_maximum_fusion.4 = bf16[256,512]{1,0:T(8,128)(2,1)S(1)} fusion(bf16[128,512]{1,0:T(8,128)(2,1)S(1)} %collective-permute-done.16, bf16[128,512]{1,0:T(8,128)(2,1)} %get-tuple-element.18), kind=kLoop, calls=%fused_computation.4 | loop fusion | flops 524288 | bytes 524288 | tf_op jit(solution)/shard_map/concatenate | solution.py:177
  12.3 0.7 collective-permute-start.17
  13.0 2.9 %collective-permute-done = bf16[1024,128]{1,0:T(8,128)(2,1)S(1)} collective-permute-done((bf16[1024,128]{1,0:T(8,128)(2,1)}, bf16[1024,128]{1,0:T(8,128)(2,1)S(1)}, u32[]{:S(2)}, u32[]{:S(2)}) %collective-permute-start) | collective-permute-done | bytes 262176 | tf_op jit(solution)/shard_map/z1/ppermute | solution.py:33
  16.0 0.1 collective-permute-start.5
  16.2 1.7 %collective-permute-start.4 = (bf16[2048,128]{1,0:T(8,128)(2,1)S(1)}, bf16[2048,128]{1,0:T(8,128)(2,1)S(1)}, u32[]{:S(2)}, u32[]{:S(2)}) collective-permute-start(bf16[2048,128]{1,0:T(8,128)(2,1)S(1)} %pad_maximum_fusion.2), channel_id=1, source_target_pairs={{0,4},{16,28},{4,8},{20,16},{8,12},{24,20},{12,0},{28,24},{1,5},{1... | collective-permute-start | bytes 1572872 | tf_op jit(solution)/shard_map/up0/ppermute | solution.py:33
  17.9 0.9 %collective-permute-done.17 = bf16[256,512]{1,0:T(8,128)(2,1)S(1)} collective-permute-done((bf16[256,512]{1,0:T(8,128)(2,1)S(1)}, bf16[256,512]{1,0:T(8,128)(2,1)S(1)}, u32[]{:S(2)}, u32[]{:S(2)}) %collective-permute-start.17) | collective-permute-done | bytes 262176 | tf_op jit(solution)/shard_map/r1/ppermute | solution.py:33
  18.8 0.1 select_select_fusion
  18.9 0.8 %collective-permute-start.18 = (bf16[256,256]{1,0:T(8,128)(2,1)S(1)}, bf16[256,256]{1,0:T(8,128)(2,1)S(1)}, u32[]{:S(2)}, u32[]{:S(2)}) collective-permute-start(bf16[256,256]{1,0:T(8,128)(2,1)S(1)} %slice.61), channel_id=1, source_target_pairs={{0,16},{16,0},{1,17},{17,1},{2,18},{18,2},{3,19},{19,3},{4,20},{20... | collective-permute-start | bytes 393224 | tf_op jit(solution)/shard_map/c1/ppermute | solution.py:33
  19.7 0.1 pad_maximum_fusion
  19.8 1.5 %collective-permute-start.6 = (bf16[4096,128]{1,0:T(8,128)(2,1)S(1)}, bf16[4096,128]{1,0:T(8,128)(2,1)S(1)}, u32[]{:S(2)}, u32[]{:S(2)}) collective-permute-start(bf16[4096,128]{1,0:T(8,128)(2,1)S(1)} %pad_maximum_fusion), channel_id=1, source_target_pairs={{0,4},{16,28},{4,8},{20,16},{8,12},{24,20},{12,0},{28,24},{1,5},{1... | collective-permute-start | bytes 3145736 | tf_op jit(solution)/shard_map/up12/ppermute | solution.py:33
  21.3 1.9 %collective-permute-start.2 = (bf16[1024,128]{1,0:T(8,128)(2,1)S(1)}, bf16[1024,128]{1,0:T(8,128)(2,1)S(1)}, u32[]{:S(2)}, u32[]{:S(2)}) collective-permute-start(bf16[1024,128]{1,0:T(8,128)(2,1)S(1)} %collective-permute-done.1), channel_id=1, source_target_pairs={{0,1},{16,17},{1,0},{17,16},{2,3},{18,19},{3,2},{19,18},{4,5},{20,... | collective-permute-start | bytes 786440 | tf_op jit(solution)/shard_map/z3/ppermute | solution.py:33
  23.3 4.6 %collective-permute-start.19 = (bf16[256,256]{1,0:T(8,128)(2,1)S(1)}, bf16[256,256]{1,0:T(8,128)(2,1)S(1)}, u32[]{:S(2)}, u32[]{:S(2)}) collective-permute-start(bf16[256,256]{1,0:T(8,128)(2,1)S(1)} %slice_add_fusion), channel_id=1, source_target_pairs={{0,32},{32,0},{1,33},{33,1},{2,34},{34,2},{3,35},{35,3},{4,36},{36... | collective-permute-start | bytes 393224 | tf_op jit(solution)/shard_map/zh/ppermute | solution.py:33
  27.9 2.4 %collective-permute-done.2.refs_2_ = bf16[1024,128]{1,0:T(8,128)(2,1)S(1)} collective-permute-done((bf16[1024,128]{1,0:T(8,128)(2,1)S(1)}, bf16[1024,128]{1,0:T(8,128)(2,1)S(1)}, u32[]{:S(2)}, u32[]{:S(2)}) %collective-permute-start.2) | collective-permute-done | bytes 262176 | tf_op jit(solution)/shard_map/z3/ppermute | solution.py:33
  30.2 0.5 collective-permute-start.11
  30.7 9.6 %collective-permute-done.19 = bf16[256,256]{1,0:T(8,128)(2,1)S(1)} collective-permute-done((bf16[256,256]{1,0:T(8,128)(2,1)S(1)}, bf16[256,256]{1,0:T(8,128)(2,1)S(1)}, u32[]{:S(2)}, u32[]{:S(2)}) %collective-permute-start.19) | collective-permute-done | bytes 131104 | tf_op jit(solution)/shard_map/zh/ppermute | solution.py:33
  40.3 0.2 collective-permute-start.20
  40.6 0.1 collective-permute-start.8
  40.7 1.1 %collective-permute-done.20 = bf16[256,256]{1,0:T(8,128)(2,1)S(1)} collective-permute-done((bf16[256,256]{1,0:T(8,128)(2,1)S(1)}, bf16[256,256]{1,0:T(8,128)(2,1)S(1)}, u32[]{:S(2)}, u32[]{:S(2)}) %collective-permute-start.20) | collective-permute-done | bytes 131104 | tf_op jit(solution)/shard_map/c2/ppermute | solution.py:33
  41.8 0.6 collective-permute-start.21
  42.4 0.2 collective-permute-start.12
  42.7 0.1 pad_maximum_fusion.1
  42.8 1.7 %collective-permute-start.7 = (bf16[3072,128]{1,0:T(8,128)(2,1)S(1)}, bf16[3072,128]{1,0:T(8,128)(2,1)S(1)}, u32[]{:S(2)}, u32[]{:S(2)}) collective-permute-start(bf16[3072,128]{1,0:T(8,128)(2,1)S(1)} %pad_maximum_fusion.1), channel_id=1, source_target_pairs={{0,16},{16,0},{1,17},{17,1},{2,18},{18,2},{3,19},{19,3},{4,20},{20... | collective-permute-start | bytes 2359304 | tf_op jit(solution)/shard_map/down/ppermute | solution.py:33
  44.5 1.3 %collective-permute-start.22 = (bf16[256,256]{1,0:T(8,128)(2,1)S(1)}, bf16[256,256]{1,0:T(8,128)(2,1)S(1)}, u32[]{:S(2)}, u32[]{:S(2)}) collective-permute-start(bf16[256,256]{1,0:T(8,128)(2,1)S(1)} %add.7), channel_id=1, source_target_pairs={{0,128},{16,144},{64,192},{80,208},{128,0},{144,16},{192,64},{208,... | collective-permute-start | bytes 393224 | tf_op jit(solution)/shard_map/g2/ppermute | solution.py:33
  45.8 2.5 %collective-permute-done.8.refs_5_ = bf16[1024,128]{1,0:T(8,128)(2,1)S(1)} collective-permute-done((bf16[1024,128]{1,0:T(8,128)(2,1)S(1)}, bf16[1024,128]{1,0:T(8,128)(2,1)S(1)}, u32[]{:S(2)}, u32[]{:S(2)}) %collective-permute-start.8) | collective-permute-done | bytes 262176 | tf_op jit(solution)/shard_map/far0/ppermute | solution.py:33
  48.2 1.0 %collective-permute-start.9 = (bf16[1024,128]{1,0:T(8,128)(2,1)S(1)}, bf16[1024,128]{1,0:T(8,128)(2,1)S(1)}, u32[]{:S(2)}, u32[]{:S(2)}) collective-permute-start(bf16[1024,128]{1,0:T(8,128)(2,1)S(1)} %collective-permute-done.8.refs_5_), channel_id=1, source_target_pairs={{0,1},{16,17},{1,0},{17,16},{2,3},{18,19},{3,2},{19,18},{4,5},{20,... | collective-permute-start | bytes 786440 | tf_op jit(solution)/shard_map/far1/ppermute | solution.py:33
  49.3 0.1 collective-permute-start.10
  49.4 2.8 %collective-permute-done.22 = bf16[256,256]{1,0:T(8,128)(2,1)S(1)} collective-permute-done((bf16[256,256]{1,0:T(8,128)(2,1)S(1)}, bf16[256,256]{1,0:T(8,128)(2,1)S(1)}, u32[]{:S(2)}, u32[]{:S(2)}) %collective-permute-start.22) | collective-permute-done | bytes 131104 | tf_op jit(solution)/shard_map/g2/ppermute | solution.py:33
  52.2 0.1 collective-permute-start.23
  52.3 1.6 %collective-permute-done.12.refs_9_ = bf16[2048,128]{1,0:T(8,128)(2,1)S(1)} collective-permute-done((bf16[2048,128]{1,0:T(8,128)(2,1)S(1)}, bf16[2048,128]{1,0:T(8,128)(2,1)S(1)}, u32[]{:S(2)}, u32[]{:S(2)}) %collective-permute-start.12) | collective-permute-done | bytes 524320 | tf_op jit(solution)/shard_map/up3/ppermute | solution.py:33
  53.9 3.1 %collective-permute-done.10.refs_8_ = bf16[1024,128]{1,0:T(8,128)(2,1)S(1)} collective-permute-done((bf16[1024,128]{1,0:T(8,128)(2,1)S(1)}, bf16[1024,128]{1,0:T(8,128)(2,1)S(1)}, u32[]{:S(2)}, u32[]{:S(2)}) %collective-permute-start.10) | collective-permute-done | bytes 262176 | tf_op jit(solution)/shard_map/far2/ppermute | solution.py:33
  57.0 7.6 %collective-permute-done.14.refs_11_ = bf16[1024,128]{1,0:T(8,128)(2,1)S(1)} collective-permute-done((bf16[1024,128]{1,0:T(8,128)(2,1)S(1)}, bf16[1024,128]{1,0:T(8,128)(2,1)S(1)}, u32[]{:S(2)}, u32[]{:S(2)}) %collective-permute-start.14) | collective-permute-done | bytes 262176 | tf_op jit(solution)/shard_map/far3/ppermute | solution.py:33
  64.6 6.2 %shard_map.48 = f32[1024,2048]{1,0:T(8,128)} custom-call(s32[48]{0:T(128)S(1)} %copy-done.1, bf16[1024,128]{1,0:T(8,128)(2,1)S(1)} %copy-done, bf16[2048,128]{1,0:T(8,128)(2,1)S(1)} %constant_dynamic-update-slice_fusion.refs_1_, bf16[1024,128]{1,0:T(8,128)(2,1)S(1)} %collective-permute-done.2.refs_2_, bf16[2048,128]{1,0:T(8,128)(2,1)S(1)} %collective-permute-done.4.refs_3_, ...), custom_call_target="tpu_custom_call" | custom-call | flops 1073741824 | bytes 8388608 | tf_op jit(solution)/shard_map/pallas_call | solution.py:263
  (39 shorter events, 0.4 us)
Async XLA Ops:
  0.0 16.2 %copy-start = (bf16[1024,128]{1,0:T(8,128)(2,1)S(1)}, bf16[1024,128]{1,0:T(8,128)(2,1)}, u32[]{:S(2)}) copy-start(bf16[1024,128]{1,0:T(8,128)(2,1)} %refs_0_.1) | copy-start | bytes 786436
  0.0 16.1 %collective-permute-start.3 = (bf16[1024,128]{1,0:T(8,128)(2,1)}, bf16[1024,128]{1,0:T(8,128)(2,1)S(1)}, u32[]{:S(2)}, u32[]{:S(2)}) collective-permute-start(bf16[1024,128]{1,0:T(8,128)(2,1)} %refs_0_.1), channel_id=1, source_target_pairs={{0,16},{16,0},{1,17},{17,1},{2,18},{18,2},{3,19},{19,3},{4,20},{20... | collective-permute-start | bytes 786440 | tf_op jit(solution)/shard_map/swap0/ppermute | solution.py:33
  0.0 16.0 %collective-permute-start.1 = (bf16[1024,128]{1,0:T(8,128)(2,1)}, bf16[1024,128]{1,0:T(8,128)(2,1)S(1)}, u32[]{:S(2)}, u32[]{:S(2)}) collective-permute-start(bf16[1024,128]{1,0:T(8,128)(2,1)} %refs_0_.1), channel_id=1, source_target_pairs={{0,2},{16,18},{1,3},{17,19},{2,0},{18,16},{3,1},{19,17},{4,6},{20,... | collective-permute-start | bytes 786440 | tf_op jit(solution)/shard_map/z2/ppermute | solution.py:33
  3.4 12.6 %collective-permute-start = (bf16[1024,128]{1,0:T(8,128)(2,1)}, bf16[1024,128]{1,0:T(8,128)(2,1)S(1)}, u32[]{:S(2)}, u32[]{:S(2)}) collective-permute-start(bf16[1024,128]{1,0:T(8,128)(2,1)} %refs_0_.1), channel_id=1, source_target_pairs={{0,1},{16,17},{1,0},{17,16},{2,3},{18,19},{3,2},{19,18},{4,5},{20,... | collective-permute-start | bytes 786440 | tf_op jit(solution)/shard_map/z1/ppermute | solution.py:33
  5.4 13.4 %copy-start.2 = (bf16[128,512]{1,0:T(8,128)(2,1)S(1)}, bf16[128,512]{1,0:T(8,128)(2,1)}, u32[]{:S(2)}) copy-start(bf16[128,512]{1,0:T(8,128)(2,1)} %get-tuple-element.20) | copy-start | bytes 393220
  5.4 13.4 %collective-permute-start.15 = (bf16[128,512]{1,0:T(8,128)(2,1)}, bf16[128,512]{1,0:T(8,128)(2,1)S(1)}, u32[]{:S(2)}, u32[]{:S(2)}) collective-permute-start(bf16[128,512]{1,0:T(8,128)(2,1)} %get-tuple-element.17), channel_id=1, source_target_pairs={{0,128},{16,144},{64,192},{80,208},{128,0},{144,16},{192,64},{208,... | collective-permute-start | bytes 393224 | tf_op jit(solution)/shard_map/r2/ppermute | solution.py:33
  8.5 2.9 %collective-permute-start.16 = (bf16[128,512]{1,0:T(8,128)(2,1)}, bf16[128,512]{1,0:T(8,128)(2,1)S(1)}, u32[]{:S(2)}, u32[]{:S(2)}) collective-permute-start(bf16[128,512]{1,0:T(8,128)(2,1)} %get-tuple-element.19), channel_id=1, source_target_pairs={{0,16},{16,0},{1,17},{17,1},{2,18},{18,2},{3,19},{19,3},{4,20},{20... | collective-permute-start | bytes 393224 | tf_op jit(solution)/shard_map/r0/ppermute | solution.py:33
  12.3 6.5 %collective-permute-start.17 = (bf16[256,512]{1,0:T(8,128)(2,1)S(1)}, bf16[256,512]{1,0:T(8,128)(2,1)S(1)}, u32[]{:S(2)}, u32[]{:S(2)}) collective-permute-start(bf16[256,512]{1,0:T(8,128)(2,1)S(1)} %pad_maximum_fusion.4), channel_id=1, source_target_pairs={{0,64},{16,208},{64,0},{80,144},{128,192},{144,80},{192,128},{208,... | collective-permute-start | bytes 786440 | tf_op jit(solution)/shard_map/r1/ppermute | solution.py:33
  16.0 3.7 %collective-permute-start.5 = (bf16[2048,128]{1,0:T(8,128)(2,1)S(1)}, bf16[2048,128]{1,0:T(8,128)(2,1)S(1)}, u32[]{:S(2)}, u32[]{:S(2)}) collective-permute-start(bf16[2048,128]{1,0:T(8,128)(2,1)S(1)} %constant_dynamic-update-slice_fusion.refs_1_), channel_id=1, source_target_pairs={{0,16},{16,0},{1,17},{17,1},{2,18},{18,2},{3,19},{19,3},{4,20},{20... | collective-permute-start | bytes 1572872 | tf_op jit(solution)/shard_map/turned/ppermute | solution.py:33
  16.2 24.3 %collective-permute-start.4 = (bf16[2048,128]{1,0:T(8,128)(2,1)S(1)}, bf16[2048,128]{1,0:T(8,128)(2,1)S(1)}, u32[]{:S(2)}, u32[]{:S(2)}) collective-permute-start(bf16[2048,128]{1,0:T(8,128)(2,1)S(1)} %pad_maximum_fusion.2), channel_id=1, source_target_pairs={{0,4},{16,28},{4,8},{20,16},{8,12},{24,20},{12,0},{28,24},{1,5},{1... | collective-permute-start | bytes 1572872 | tf_op jit(solution)/shard_map/up0/ppermute | solution.py:33
  18.9 4.3 %collective-permute-start.18 = (bf16[256,256]{1,0:T(8,128)(2,1)S(1)}, bf16[256,256]{1,0:T(8,128)(2,1)S(1)}, u32[]{:S(2)}, u32[]{:S(2)}) collective-permute-start(bf16[256,256]{1,0:T(8,128)(2,1)S(1)} %slice.61), channel_id=1, source_target_pairs={{0,16},{16,0},{1,17},{17,1},{2,18},{18,2},{3,19},{19,3},{4,20},{20... | collective-permute-start | bytes 393224 | tf_op jit(solution)/shard_map/c1/ppermute | solution.py:33
  19.8 22.6 %collective-permute-start.6 = (bf16[4096,128]{1,0:T(8,128)(2,1)S(1)}, bf16[4096,128]{1,0:T(8,128)(2,1)S(1)}, u32[]{:S(2)}, u32[]{:S(2)}) collective-permute-start(bf16[4096,128]{1,0:T(8,128)(2,1)S(1)} %pad_maximum_fusion), channel_id=1, source_target_pairs={{0,4},{16,28},{4,8},{20,16},{8,12},{24,20},{12,0},{28,24},{1,5},{1... | collective-permute-start | bytes 3145736 | tf_op jit(solution)/shard_map/up12/ppermute | solution.py:33
  21.3 8.9 %collective-permute-start.2 = (bf16[1024,128]{1,0:T(8,128)(2,1)S(1)}, bf16[1024,128]{1,0:T(8,128)(2,1)S(1)}, u32[]{:S(2)}, u32[]{:S(2)}) collective-permute-start(bf16[1024,128]{1,0:T(8,128)(2,1)S(1)} %collective-permute-done.1), channel_id=1, source_target_pairs={{0,1},{16,17},{1,0},{17,16},{2,3},{18,19},{3,2},{19,18},{4,5},{20,... | collective-permute-start | bytes 786440 | tf_op jit(solution)/shard_map/z3/ppermute | solution.py:33
  23.3 17.0 %collective-permute-start.19 = (bf16[256,256]{1,0:T(8,128)(2,1)S(1)}, bf16[256,256]{1,0:T(8,128)(2,1)S(1)}, u32[]{:S(2)}, u32[]{:S(2)}) collective-permute-start(bf16[256,256]{1,0:T(8,128)(2,1)S(1)} %slice_add_fusion), channel_id=1, source_target_pairs={{0,32},{32,0},{1,33},{33,1},{2,34},{34,2},{3,35},{35,3},{4,36},{36... | collective-permute-start | bytes 393224 | tf_op jit(solution)/shard_map/zh/ppermute | solution.py:33
  30.2 12.2 %collective-permute-start.11 = (bf16[1024,128]{1,0:T(8,128)(2,1)S(1)}, bf16[1024,128]{1,0:T(8,128)(2,1)S(1)}, u32[]{:S(2)}, u32[]{:S(2)}) collective-permute-start(bf16[1024,128]{1,0:T(8,128)(2,1)S(1)} %collective-permute-done.2.refs_2_), channel_id=1, source_target_pairs={{0,16},{16,0},{1,17},{17,1},{2,18},{18,2},{3,19},{19,3},{4,20},{20... | collective-permute-start | bytes 786440 | tf_op jit(solution)/shard_map/swap3/ppermute | solution.py:33
  40.3 1.4 %collective-permute-start.20 = (bf16[256,256]{1,0:T(8,128)(2,1)S(1)}, bf16[256,256]{1,0:T(8,128)(2,1)S(1)}, u32[]{:S(2)}, u32[]{:S(2)}) collective-permute-start(bf16[256,256]{1,0:T(8,128)(2,1)S(1)} %add.7), channel_id=1, source_target_pairs={{0,16},{16,0},{1,17},{17,1},{2,18},{18,2},{3,19},{19,3},{4,20},{20... | collective-permute-start | bytes 393224 | tf_op jit(solution)/shard_map/c2/ppermute | solution.py:33
  40.6 7.7 %collective-permute-start.8 = (bf16[1024,128]{1,0:T(8,128)(2,1)S(1)}, bf16[1024,128]{1,0:T(8,128)(2,1)S(1)}, u32[]{:S(2)}, u32[]{:S(2)}) collective-permute-start(bf16[1024,128]{1,0:T(8,128)(2,1)S(1)} %get-tuple-element.25), channel_id=1, source_target_pairs={{0,4},{16,28},{4,8},{20,16},{8,12},{24,20},{12,0},{28,24},{1,5},{1... | collective-permute-start | bytes 786440 | tf_op jit(solution)/shard_map/far0/ppermute | solution.py:33
  41.8 7.5 %collective-permute-start.21 = (bf16[512,256]{1,0:T(8,128)(2,1)S(1)}, bf16[512,256]{1,0:T(8,128)(2,1)S(1)}, u32[]{:S(2)}, u32[]{:S(2)}) collective-permute-start(bf16[512,256]{1,0:T(8,128)(2,1)S(1)} %pad_maximum_fusion.5.refs_12_), channel_id=1, source_target_pairs={{0,64},{16,208},{64,0},{80,144},{128,192},{144,80},{192,128},{208,... | collective-permute-start | bytes 786440 | tf_op jit(solution)/shard_map/g1/ppermute | solution.py:33
  42.4 11.4 %collective-permute-start.12 = (bf16[2048,128]{1,0:T(8,128)(2,1)S(1)}, bf16[2048,128]{1,0:T(8,128)(2,1)S(1)}, u32[]{:S(2)}, u32[]{:S(2)}) collective-permute-start(bf16[2048,128]{1,0:T(8,128)(2,1)S(1)} %pad_maximum_fusion.3), channel_id=1, source_target_pairs={{0,4},{16,28},{4,8},{20,16},{8,12},{24,20},{12,0},{28,24},{1,5},{1... | collective-permute-start | bytes 1572872 | tf_op jit(solution)/shard_map/up3/ppermute | solution.py:33
  42.7 21.9 %copy-start.1 = (s32[48]{0:T(128)S(1)}, s32[48]{0:T(128)}, u32[]{:S(2)}) copy-start(s32[48]{0:T(128)} %shard_map.46.table) | copy-start | bytes 580
  42.8 21.8 %collective-permute-start.7 = (bf16[3072,128]{1,0:T(8,128)(2,1)S(1)}, bf16[3072,128]{1,0:T(8,128)(2,1)S(1)}, u32[]{:S(2)}, u32[]{:S(2)}) collective-permute-start(bf16[3072,128]{1,0:T(8,128)(2,1)S(1)} %pad_maximum_fusion.1), channel_id=1, source_target_pairs={{0,16},{16,0},{1,17},{17,1},{2,18},{18,2},{3,19},{19,3},{4,20},{20... | collective-permute-start | bytes 2359304 | tf_op jit(solution)/shard_map/down/ppermute | solution.py:33
  44.5 7.7 %collective-permute-start.22 = (bf16[256,256]{1,0:T(8,128)(2,1)S(1)}, bf16[256,256]{1,0:T(8,128)(2,1)S(1)}, u32[]{:S(2)}, u32[]{:S(2)}) collective-permute-start(bf16[256,256]{1,0:T(8,128)(2,1)S(1)} %add.7), channel_id=1, source_target_pairs={{0,128},{16,144},{64,192},{80,208},{128,0},{144,16},{192,64},{208,... | collective-permute-start | bytes 393224 | tf_op jit(solution)/shard_map/g2/ppermute | solution.py:33
  48.2 8.7 %collective-permute-start.9 = (bf16[1024,128]{1,0:T(8,128)(2,1)S(1)}, bf16[1024,128]{1,0:T(8,128)(2,1)S(1)}, u32[]{:S(2)}, u32[]{:S(2)}) collective-permute-start(bf16[1024,128]{1,0:T(8,128)(2,1)S(1)} %collective-permute-done.8.refs_5_), channel_id=1, source_target_pairs={{0,1},{16,17},{1,0},{17,16},{2,3},{18,19},{3,2},{19,18},{4,5},{20,... | collective-permute-start | bytes 786440 | tf_op jit(solution)/shard_map/far1/ppermute | solution.py:33
  49.3 7.7 %collective-permute-start.10 = (bf16[1024,128]{1,0:T(8,128)(2,1)S(1)}, bf16[1024,128]{1,0:T(8,128)(2,1)S(1)}, u32[]{:S(2)}, u32[]{:S(2)}) collective-permute-start(bf16[1024,128]{1,0:T(8,128)(2,1)S(1)} %slice.55), channel_id=1, source_target_pairs={{0,4},{16,28},{4,8},{20,16},{8,12},{24,20},{12,0},{28,24},{1,5},{1... | collective-permute-start | bytes 786440 | tf_op jit(solution)/shard_map/far2/ppermute | solution.py:33
  52.2 4.8 %collective-permute-start.23 = (bf16[768,256]{1,0:T(8,128)(2,1)S(1)}, bf16[768,256]{1,0:T(8,128)(2,1)S(1)}, u32[]{:S(2)}, u32[]{:S(2)}) collective-permute-start(bf16[768,256]{1,0:T(8,128)(2,1)S(1)} %constant_dynamic-update-slice_fusion.2.refs_13_), channel_id=1, source_target_pairs={{0,16},{16,0},{1,17},{17,1},{2,18},{18,2},{3,19},{19,3},{4,20},{20... | collective-permute-start | bytes 1179656 | tf_op jit(solution)/shard_map/c34/ppermute | solution.py:33
  57.0 7.6 %collective-permute-start.14 = (bf16[1024,128]{1,0:T(8,128)(2,1)S(1)}, bf16[1024,128]{1,0:T(8,128)(2,1)S(1)}, u32[]{:S(2)}, u32[]{:S(2)}) collective-permute-start(bf16[1024,128]{1,0:T(8,128)(2,1)S(1)} %get-tuple-element.16), channel_id=1, source_target_pairs={{0,4},{16,28},{4,8},{20,16},{8,12},{24,20},{12,0},{28,24},{1,5},{1... | collective-permute-start | bytes 786440 | tf_op jit(solution)/shard_map/far3/ppermute | solution.py:33
  57.0 7.6 %collective-permute-start.13 = (bf16[1024,128]{1,0:T(8,128)(2,1)S(1)}, bf16[1024,128]{1,0:T(8,128)(2,1)S(1)}, u32[]{:S(2)}, u32[]{:S(2)}) collective-permute-start(bf16[1024,128]{1,0:T(8,128)(2,1)S(1)} %get-tuple-element.24), channel_id=1, source_target_pairs={{0,16},{16,0},{1,17},{17,1},{2,18},{18,2},{3,19},{19,3},{4,20},{20... | collective-permute-start | bytes 786440 | tf_op jit(solution)/shard_map/down3/ppermute | solution.py:33

commit v4 on v3

--- a/solution.py
+++ b/solution.py
@@ -194,14 +194,14 @@
     moved = send("zh", part, "zh", [(0, 1), (1, 0)], turned)
     part = part + moved
     far1 = cross_z("far1", far0, (1, 1))
-    far2 = ring("far2", up12[rows : 2 * rows])
 
     pair = doubled("c2", part)
     near = cross_x("g1", pair, (1, 3), moved)
     across = cross_x("g2", part, (2, 2))
     down = jnp.concatenate([up0[rows:], up12[2 * rows :]])
     down = swap("down", down)
-    far3 = ring("far3", up3[:rows], far2)
+    both_far = jnp.concatenate([up12[rows : 2 * rows], up3[:rows]])
+    far23 = ring("far23", both_far)
     down3 = swap("down3", up3[rows:])
     both = jnp.concatenate([near, across])
     both_swapped = swap("c34", both)
@@ -209,8 +209,8 @@
     pieces = [(own, 0), (line, 0), (line, rows), (z3, 0)]
     pieces += [(up0, 0), (down, 0), (far0, 0)]
     pieces += [(up12, 0), (down, rows), (far1, 0)]
-    pieces += [(up12, rows), (down, 2 * rows), (far2, 0)]
-    pieces += [(up3, 0), (down3, 0), (far3, 0)]
+    pieces += [(up12, rows), (down, 2 * rows), (far23, 0)]
+    pieces += [(up3, 0), (down3, 0), (far23, rows)]
     return table, pieces, parts
 
 

time: 71.1 us -> 68.9 us (0.969)
  the two profiles are of different devices: /device:TPU:32 before, /device:TPU:1 now
where the time goes in v4:
time: 68.9 us; the launch traced here: 68.7 us
  starting transfers between devices  34 us (49%)
  waiting for transfers between devices  21.7 us (31%)
  Pallas kernels  9.6 us (14%)
  other arithmetic  2.07 us (3%)
  local copies, waits for them, and re-layouts  0.91 us (1%)
    ppermute x23, starting transfers between devices, send(): return lax.ppermute(value, axes, pairs)  34 us
    ppermute x23, waiting for transfers between devices, send(): return lax.ppermute(value, axes, pairs)  21.7 us
    pallas_call x1, Pallas kernels, multiply(): pl.pallas_call(functools.partial(multiply_kernel, tuple(spots)), out_shap...  6.22 us
    pallas_call x1, Pallas kernels, cut(): pl.pallas_call(cut_kernel, out_shape=[shape] * NX, in_specs=[ANY], out_sp...  1.92 us
    pallas_call x1, Pallas kernels, make_table(): pl.pallas_call(table_kernel, out_shape=jax.ShapeDtypeStruct((TABLE,), jnp...  1.45 us
  transfers between devices with their start and end apart: 23, of which 8 were waited for; matrix products, arithmetic and copies ran while one was open for 4% of the time, Pallas kernels for 5%

profile of v4, /device:TPU:1, one launch (start us, length us, event | category | flops | bytes accessed | tf_op | source)
XLA Modules:
  0.0 68.7 jit_solution(4481550334335263600)
XLA Ops:
  0.0 3.2 %collective-permute-start.3 = (bf16[1024,128]{1,0:T(8,128)(2,1)}, bf16[1024,128]{1,0:T(8,128)(2,1)S(1)}, u32[]{:S(2)}, u32[]{:S(2)}) collective-permute-start(bf16[1024,128]{1,0:T(8,128)(2,1)} %refs_0_.1), channel_id=1, source_target_pairs={{0,16},{16,0},{1,17},{17,1},{2,18},{18,2},{3,19},{19,3},{4,20},{20... | collective-permute-start | bytes 786440 | tf_op jit(solution)/shard_map/swap0/ppermute | solution.py:33
  3.2 1.3 %collective-permute-start.1 = (bf16[1024,128]{1,0:T(8,128)(2,1)}, bf16[1024,128]{1,0:T(8,128)(2,1)S(1)}, u32[]{:S(2)}, u32[]{:S(2)}) collective-permute-start(bf16[1024,128]{1,0:T(8,128)(2,1)} %refs_0_.1), channel_id=1, source_target_pairs={{0,2},{16,18},{1,3},{17,19},{2,0},{18,16},{3,1},{19,17},{4,6},{20,... | collective-permute-start | bytes 786440 | tf_op jit(solution)/shard_map/z2/ppermute | solution.py:33
  4.5 1.6 %collective-permute-start = (bf16[1024,128]{1,0:T(8,128)(2,1)}, bf16[1024,128]{1,0:T(8,128)(2,1)S(1)}, u32[]{:S(2)}, u32[]{:S(2)}) collective-permute-start(bf16[1024,128]{1,0:T(8,128)(2,1)} %refs_0_.1), channel_id=1, source_target_pairs={{0,1},{16,17},{1,0},{17,16},{2,3},{18,19},{3,2},{19,18},{4,5},{20,... | collective-permute-start | bytes 786440 | tf_op jit(solution)/shard_map/z1/ppermute | solution.py:33
  6.1 1.9 %shard_map.47 = (bf16[128,512]{1,0:T(8,128)(2,1)}, bf16[128,512]{1,0:T(8,128)(2,1)}, bf16[128,512]{1,0:T(8,128)(2,1)}, bf16[128,512]{1,0:T(8,128)(2,1)}) custom-call(bf16[128,2048]{1,0:T(8,128)(2,1)} %integrals.1), custom_call_target="tpu_custom_call" | custom-call | tf_op jit(solution)/shard_map/pallas_call | solution.py:147
  8.1 2.8 %collective-permute-start.14 = (bf16[128,512]{1,0:T(8,128)(2,1)}, bf16[128,512]{1,0:T(8,128)(2,1)S(1)}, u32[]{:S(2)}, u32[]{:S(2)}) collective-permute-start(bf16[128,512]{1,0:T(8,128)(2,1)} %get-tuple-element.15), channel_id=1, source_target_pairs={{0,128},{16,144},{64,192},{80,208},{128,0},{144,16},{192,64},{208,... | collective-permute-start | bytes 393224 | tf_op jit(solution)/shard_map/r2/ppermute | solution.py:33
  10.9 0.8 %collective-permute-start.15 = (bf16[128,512]{1,0:T(8,128)(2,1)}, bf16[128,512]{1,0:T(8,128)(2,1)S(1)}, u32[]{:S(2)}, u32[]{:S(2)}) collective-permute-start(bf16[128,512]{1,0:T(8,128)(2,1)} %get-tuple-element.17), channel_id=1, source_target_pairs={{0,16},{16,0},{1,17},{17,1},{2,18},{18,2},{3,19},{19,3},{4,20},{20... | collective-permute-start | bytes 393224 | tf_op jit(solution)/shard_map/r0/ppermute | solution.py:33
  11.7 1.5 %shard_map.46.table = s32[48]{0:T(128)} custom-call(s32[16]{0:T(128)} %contract.1, s32[16]{0:T(128)} %column.1), custom_call_target="tpu_custom_call" | custom-call | tf_op jit(solution)/shard_map/pallas_call | solution.py:112
  13.2 0.7 %broadcast_compare_fusion.3 = (pred[8]{0:T(512)(128)(4,1)S(1)}, pred[8]{0:T(512)(128)(4,1)S(1)}, pred[8]{0:T(512)(128)(4,1)S(1)}, pred[8]{0:T(512)(128)(4,1)S(1)}) fusion(s32[48]{0:T(128)} %shard_map.46.table), kind=kLoop, calls=%fused_computation.24 | loop fusion | flops 32 | bytes 64 | tf_op jit(solution)/shard_map/eq | solution.py:161
  13.9 0.1 eq.74
  14.0 0.1 eq.82
  14.1 0.1 broadcast_bitcast_fusion.1
  14.2 0.1 eq.86
  14.3 0.1 broadcast_bitcast_fusion
  14.4 0.1 broadcast_bitcast_fusion.3
  14.4 0.1 eq.78
  14.5 1.0 %pad_maximum_fusion.5 = bf16[256,512]{1,0:T(8,128)(2,1)S(1)} fusion(bf16[128,512]{1,0:T(8,128)(2,1)S(1)} %collective-permute-done.15, bf16[128,512]{1,0:T(8,128)(2,1)} %get-tuple-element.16), kind=kLoop, calls=%fused_computation.5 | loop fusion | flops 524288 | bytes 524288 | tf_op jit(solution)/shard_map/concatenate | solution.py:177
  15.5 0.9 %collective-permute-start.16 = (bf16[256,512]{1,0:T(8,128)(2,1)S(1)}, bf16[256,512]{1,0:T(8,128)(2,1)S(1)}, u32[]{:S(2)}, u32[]{:S(2)}) collective-permute-start(bf16[256,512]{1,0:T(8,128)(2,1)S(1)} %pad_maximum_fusion.5), channel_id=1, source_target_pairs={{0,64},{16,208},{64,0},{80,144},{128,192},{144,80},{192,128},{208,... | collective-permute-start | bytes 786440 | tf_op jit(solution)/shard_map/r1/ppermute | solution.py:33
  16.5 0.0 copy-start
  16.5 1.5 %collective-permute-done.1 = bf16[1024,128]{1,0:T(8,128)(2,1)S(1)} collective-permute-done((bf16[1024,128]{1,0:T(8,128)(2,1)}, bf16[1024,128]{1,0:T(8,128)(2,1)S(1)}, u32[]{:S(2)}, u32[]{:S(2)}) %collective-permute-start.1) | collective-permute-done | bytes 262176 | tf_op jit(solution)/shard_map/z2/ppermute | solution.py:33
  18.0 1.0 %collective-permute-start.5 = (bf16[2048,128]{1,0:T(8,128)(2,1)S(1)}, bf16[2048,128]{1,0:T(8,128)(2,1)S(1)}, u32[]{:S(2)}, u32[]{:S(2)}) collective-permute-start(bf16[2048,128]{1,0:T(8,128)(2,1)S(1)} %constant_dynamic-update-slice_fusion.refs_1_), channel_id=1, source_target_pairs={{0,16},{16,0},{1,17},{17,1},{2,18},{18,2},{3,19},{19,3},{4,20},{20... | collective-permute-start | bytes 1572872 | tf_op jit(solution)/shard_map/turned/ppermute | solution.py:33
  19.1 0.1 broadcast_bitcast_fusion.2
  19.2 0.3 collective-permute-start.2
  19.4 2.6 %collective-permute-done.16 = bf16[256,512]{1,0:T(8,128)(2,1)S(1)} collective-permute-done((bf16[256,512]{1,0:T(8,128)(2,1)S(1)}, bf16[256,512]{1,0:T(8,128)(2,1)S(1)}, u32[]{:S(2)}, u32[]{:S(2)}) %collective-permute-start.16) | collective-permute-done | bytes 262176 | tf_op jit(solution)/shard_map/r1/ppermute | solution.py:33
  22.0 0.1 pad_maximum_fusion
  22.1 2.8 %collective-permute-start.6 = (bf16[4096,128]{1,0:T(8,128)(2,1)S(1)}, bf16[4096,128]{1,0:T(8,128)(2,1)S(1)}, u32[]{:S(2)}, u32[]{:S(2)}) collective-permute-start(bf16[4096,128]{1,0:T(8,128)(2,1)S(1)} %pad_maximum_fusion), channel_id=1, source_target_pairs={{0,4},{16,28},{4,8},{20,16},{8,12},{24,20},{12,0},{28,24},{1,5},{1... | collective-permute-start | bytes 3145736 | tf_op jit(solution)/shard_map/up12/ppermute | solution.py:33
  24.9 0.1 select_select_fusion
  25.0 0.1 collective-permute-start.17
  25.2 0.5 collective-permute-start.4
  25.7 1.4 %collective-permute-done.2.refs_2_ = bf16[1024,128]{1,0:T(8,128)(2,1)S(1)} collective-permute-done((bf16[1024,128]{1,0:T(8,128)(2,1)S(1)}, bf16[1024,128]{1,0:T(8,128)(2,1)S(1)}, u32[]{:S(2)}, u32[]{:S(2)}) %collective-permute-start.2) | collective-permute-done | bytes 262176 | tf_op jit(solution)/shard_map/z3/ppermute | solution.py:33
  27.2 0.8 %collective-permute-start.10 = (bf16[1024,128]{1,0:T(8,128)(2,1)S(1)}, bf16[1024,128]{1,0:T(8,128)(2,1)S(1)}, u32[]{:S(2)}, u32[]{:S(2)}) collective-permute-start(bf16[1024,128]{1,0:T(8,128)(2,1)S(1)} %collective-permute-done.2.refs_2_), channel_id=1, source_target_pairs={{0,16},{16,0},{1,17},{17,1},{2,18},{18,2},{3,19},{19,3},{4,20},{20... | collective-permute-start | bytes 786440 | tf_op jit(solution)/shard_map/swap3/ppermute | solution.py:33
  28.0 5.0 %collective-permute-start.18 = (bf16[256,256]{1,0:T(8,128)(2,1)S(1)}, bf16[256,256]{1,0:T(8,128)(2,1)S(1)}, u32[]{:S(2)}, u32[]{:S(2)}) collective-permute-start(bf16[256,256]{1,0:T(8,128)(2,1)S(1)} %slice_add_fusion), channel_id=1, source_target_pairs={{0,32},{32,0},{1,33},{33,1},{2,34},{34,2},{3,35},{35,3},{4,36},{36... | collective-permute-start | bytes 393224 | tf_op jit(solution)/shard_map/zh/ppermute | solution.py:33
  33.0 4.1 %collective-permute-done.18 = bf16[256,256]{1,0:T(8,128)(2,1)S(1)} collective-permute-done((bf16[256,256]{1,0:T(8,128)(2,1)S(1)}, bf16[256,256]{1,0:T(8,128)(2,1)S(1)}, u32[]{:S(2)}, u32[]{:S(2)}) %collective-permute-start.18) | collective-permute-done | bytes 131104 | tf_op jit(solution)/shard_map/zh/ppermute | solution.py:33
  37.2 1.0 %collective-permute-start.19 = (bf16[256,256]{1,0:T(8,128)(2,1)S(1)}, bf16[256,256]{1,0:T(8,128)(2,1)S(1)}, u32[]{:S(2)}, u32[]{:S(2)}) collective-permute-start(bf16[256,256]{1,0:T(8,128)(2,1)S(1)} %add.7), channel_id=1, source_target_pairs={{0,16},{16,0},{1,17},{17,1},{2,18},{18,2},{3,19},{19,3},{4,20},{20... | collective-permute-start | bytes 393224 | tf_op jit(solution)/shard_map/c2/ppermute | solution.py:33
  38.2 2.4 %collective-permute-start.11 = (bf16[2048,128]{1,0:T(8,128)(2,1)S(1)}, bf16[2048,128]{1,0:T(8,128)(2,1)S(1)}, u32[]{:S(2)}, u32[]{:S(2)}) collective-permute-start(bf16[2048,128]{1,0:T(8,128)(2,1)S(1)} %pad_maximum_fusion.3), channel_id=1, source_target_pairs={{0,4},{16,28},{4,8},{20,16},{8,12},{24,20},{12,0},{28,24},{1,5},{1... | collective-permute-start | bytes 1572872 | tf_op jit(solution)/shard_map/up3/ppermute | solution.py:33
  40.5 1.8 %collective-permute-done.4.refs_3_ = bf16[2048,128]{1,0:T(8,128)(2,1)S(1)} collective-permute-done((bf16[2048,128]{1,0:T(8,128)(2,1)S(1)}, bf16[2048,128]{1,0:T(8,128)(2,1)S(1)}, u32[]{:S(2)}, u32[]{:S(2)}) %collective-permute-start.4) | collective-permute-done | bytes 524320 | tf_op jit(solution)/shard_map/up0/ppermute | solution.py:33
  42.3 3.2 %collective-permute-start.8 = (bf16[1024,128]{1,0:T(8,128)(2,1)S(1)}, bf16[1024,128]{1,0:T(8,128)(2,1)S(1)}, u32[]{:S(2)}, u32[]{:S(2)}) collective-permute-start(bf16[1024,128]{1,0:T(8,128)(2,1)S(1)} %get-tuple-element.23), channel_id=1, source_target_pairs={{0,4},{16,28},{4,8},{20,16},{8,12},{24,20},{12,0},{28,24},{1,5},{1... | collective-permute-start | bytes 786440 | tf_op jit(solution)/shard_map/far0/ppermute | solution.py:33
  45.5 0.2 collective-permute-start.21
  45.8 1.7 %collective-permute-start.20 = (bf16[512,256]{1,0:T(8,128)(2,1)S(1)}, bf16[512,256]{1,0:T(8,128)(2,1)S(1)}, u32[]{:S(2)}, u32[]{:S(2)}) collective-permute-start(bf16[512,256]{1,0:T(8,128)(2,1)S(1)} %pad_maximum_fusion.6.refs_11_), channel_id=1, source_target_pairs={{0,64},{16,208},{64,0},{80,144},{128,192},{144,80},{192,128},{208,... | collective-permute-start | bytes 786440 | tf_op jit(solution)/shard_map/g1/ppermute | solution.py:33
  47.5 0.1 pad_maximum_fusion.1
  47.5 0.3 collective-permute-start.7
  47.8 0.1 collective-permute-done.11.refs_9_
  48.0 3.2 %collective-permute-start.12 = (bf16[2048,128]{1,0:T(8,128)(2,1)S(1)}, bf16[2048,128]{1,0:T(8,128)(2,1)S(1)}, u32[]{:S(2)}, u32[]{:S(2)}) collective-permute-start(bf16[2048,128]{1,0:T(8,128)(2,1)S(1)} %pad_maximum_fusion.4), channel_id=1, source_target_pairs={{0,4},{16,28},{4,8},{20,16},{8,12},{24,20},{12,0},{28,24},{1,5},{1... | collective-permute-start | bytes 1572872 | tf_op jit(solution)/shard_map/far23/ppermute | solution.py:33
  51.2 3.4 %collective-permute-done.20 = bf16[512,256]{1,0:T(8,128)(2,1)S(1)} collective-permute-done((bf16[512,256]{1,0:T(8,128)(2,1)S(1)}, bf16[512,256]{1,0:T(8,128)(2,1)S(1)}, u32[]{:S(2)}, u32[]{:S(2)}) %collective-permute-start.20) | collective-permute-done | bytes 262176 | tf_op jit(solution)/shard_map/g1/ppermute | solution.py:33
  54.6 0.1 collective-permute-start.22
  54.7 0.3 collective-permute-start.9
  55.0 0.4 collective-permute-start.13
  55.4 6.8 %collective-permute-done.9.refs_7_ = bf16[1024,128]{1,0:T(8,128)(2,1)S(1)} collective-permute-done((bf16[1024,128]{1,0:T(8,128)(2,1)S(1)}, bf16[1024,128]{1,0:T(8,128)(2,1)S(1)}, u32[]{:S(2)}, u32[]{:S(2)}) %collective-permute-start.9) | collective-permute-done | bytes 262176 | tf_op jit(solution)/shard_map/far1/ppermute | solution.py:33
  62.3 6.2 %shard_map.48 = f32[1024,2048]{1,0:T(8,128)} custom-call(s32[48]{0:T(128)S(1)} %copy-done.1, bf16[1024,128]{1,0:T(8,128)(2,1)S(1)} %copy-done, bf16[2048,128]{1,0:T(8,128)(2,1)S(1)} %constant_dynamic-update-slice_fusion.refs_1_, bf16[1024,128]{1,0:T(8,128)(2,1)S(1)} %collective-permute-done.2.refs_2_, bf16[2048,128]{1,0:T(8,128)(2,1)S(1)} %collective-permute-done.4.refs_3_, ...), custom_call_target="tpu_custom_call" | custom-call | flops 1073741824 | bytes 8388608 | tf_op jit(solution)/shard_map/pallas_call | solution.py:263
  (38 shorter events, 0.5 us)
Async XLA Ops:
  0.0 25.1 %collective-permute-start.3 = (bf16[1024,128]{1,0:T(8,128)(2,1)}, bf16[1024,128]{1,0:T(8,128)(2,1)S(1)}, u32[]{:S(2)}, u32[]{:S(2)}) collective-permute-start(bf16[1024,128]{1,0:T(8,128)(2,1)} %refs_0_.1), channel_id=1, source_target_pairs={{0,16},{16,0},{1,17},{17,1},{2,18},{18,2},{3,19},{19,3},{4,20},{20... | collective-permute-start | bytes 786440 | tf_op jit(solution)/shard_map/swap0/ppermute | solution.py:33
  3.2 14.8 %collective-permute-start.1 = (bf16[1024,128]{1,0:T(8,128)(2,1)}, bf16[1024,128]{1,0:T(8,128)(2,1)S(1)}, u32[]{:S(2)}, u32[]{:S(2)}) collective-permute-start(bf16[1024,128]{1,0:T(8,128)(2,1)} %refs_0_.1), channel_id=1, source_target_pairs={{0,2},{16,18},{1,3},{17,19},{2,0},{18,16},{3,1},{19,17},{4,6},{20,... | collective-permute-start | bytes 786440 | tf_op jit(solution)/shard_map/z2/ppermute | solution.py:33
  4.5 11.9 %collective-permute-start = (bf16[1024,128]{1,0:T(8,128)(2,1)}, bf16[1024,128]{1,0:T(8,128)(2,1)S(1)}, u32[]{:S(2)}, u32[]{:S(2)}) collective-permute-start(bf16[1024,128]{1,0:T(8,128)(2,1)} %refs_0_.1), channel_id=1, source_target_pairs={{0,1},{16,17},{1,0},{17,16},{2,3},{18,19},{3,2},{19,18},{4,5},{20,... | collective-permute-start | bytes 786440 | tf_op jit(solution)/shard_map/z1/ppermute | solution.py:33
  8.1 16.9 %collective-permute-start.14 = (bf16[128,512]{1,0:T(8,128)(2,1)}, bf16[128,512]{1,0:T(8,128)(2,1)S(1)}, u32[]{:S(2)}, u32[]{:S(2)}) collective-permute-start(bf16[128,512]{1,0:T(8,128)(2,1)} %get-tuple-element.15), channel_id=1, source_target_pairs={{0,128},{16,144},{64,192},{80,208},{128,0},{144,16},{192,64},{208,... | collective-permute-start | bytes 393224 | tf_op jit(solution)/shard_map/r2/ppermute | solution.py:33
  10.9 3.6 %collective-permute-start.15 = (bf16[128,512]{1,0:T(8,128)(2,1)}, bf16[128,512]{1,0:T(8,128)(2,1)S(1)}, u32[]{:S(2)}, u32[]{:S(2)}) collective-permute-start(bf16[128,512]{1,0:T(8,128)(2,1)} %get-tuple-element.17), channel_id=1, source_target_pairs={{0,16},{16,0},{1,17},{17,1},{2,18},{18,2},{3,19},{19,3},{4,20},{20... | collective-permute-start | bytes 393224 | tf_op jit(solution)/shard_map/r0/ppermute | solution.py:33
  14.5 10.4 %copy-start.2 = (bf16[128,512]{1,0:T(8,128)(2,1)S(1)}, bf16[128,512]{1,0:T(8,128)(2,1)}, u32[]{:S(2)}) copy-start(bf16[128,512]{1,0:T(8,128)(2,1)} %get-tuple-element.18) | copy-start | bytes 393220
  15.5 6.5 %collective-permute-start.16 = (bf16[256,512]{1,0:T(8,128)(2,1)S(1)}, bf16[256,512]{1,0:T(8,128)(2,1)S(1)}, u32[]{:S(2)}, u32[]{:S(2)}) collective-permute-start(bf16[256,512]{1,0:T(8,128)(2,1)S(1)} %pad_maximum_fusion.5), channel_id=1, source_target_pairs={{0,64},{16,208},{64,0},{80,144},{128,192},{144,80},{192,128},{208,... | collective-permute-start | bytes 786440 | tf_op jit(solution)/shard_map/r1/ppermute | solution.py:33
  16.5 8.7 %copy-start = (bf16[1024,128]{1,0:T(8,128)(2,1)S(1)}, bf16[1024,128]{1,0:T(8,128)(2,1)}, u32[]{:S(2)}) copy-start(bf16[1024,128]{1,0:T(8,128)(2,1)} %refs_0_.1) | copy-start | bytes 786436
  18.0 4.0 %collective-permute-start.5 = (bf16[2048,128]{1,0:T(8,128)(2,1)S(1)}, bf16[2048,128]{1,0:T(8,128)(2,1)S(1)}, u32[]{:S(2)}, u32[]{:S(2)}) collective-permute-start(bf16[2048,128]{1,0:T(8,128)(2,1)S(1)} %constant_dynamic-update-slice_fusion.refs_1_), channel_id=1, source_target_pairs={{0,16},{16,0},{1,17},{17,1},{2,18},{18,2},{3,19},{19,3},{4,20},{20... | collective-permute-start | bytes 1572872 | tf_op jit(solution)/shard_map/turned/ppermute | solution.py:33
  19.2 8.0 %collective-permute-start.2 = (bf16[1024,128]{1,0:T(8,128)(2,1)S(1)}, bf16[1024,128]{1,0:T(8,128)(2,1)S(1)}, u32[]{:S(2)}, u32[]{:S(2)}) collective-permute-start(bf16[1024,128]{1,0:T(8,128)(2,1)S(1)} %collective-permute-done.1), channel_id=1, source_target_pairs={{0,1},{16,17},{1,0},{17,16},{2,3},{18,19},{3,2},{19,18},{4,5},{20,... | collective-permute-start | bytes 786440 | tf_op jit(solution)/shard_map/z3/ppermute | solution.py:33
  22.1 16.1 %collective-permute-start.6 = (bf16[4096,128]{1,0:T(8,128)(2,1)S(1)}, bf16[4096,128]{1,0:T(8,128)(2,1)S(1)}, u32[]{:S(2)}, u32[]{:S(2)}) collective-permute-start(bf16[4096,128]{1,0:T(8,128)(2,1)S(1)} %pad_maximum_fusion), channel_id=1, source_target_pairs={{0,4},{16,28},{4,8},{20,16},{8,12},{24,20},{12,0},{28,24},{1,5},{1... | collective-permute-start | bytes 3145736 | tf_op jit(solution)/shard_map/up12/ppermute | solution.py:33
  25.0 2.9 %collective-permute-start.17 = (bf16[256,256]{1,0:T(8,128)(2,1)S(1)}, bf16[256,256]{1,0:T(8,128)(2,1)S(1)}, u32[]{:S(2)}, u32[]{:S(2)}) collective-permute-start(bf16[256,256]{1,0:T(8,128)(2,1)S(1)} %slice.61), channel_id=1, source_target_pairs={{0,16},{16,0},{1,17},{17,1},{2,18},{18,2},{3,19},{19,3},{4,20},{20... | collective-permute-start | bytes 393224 | tf_op jit(solution)/shard_map/c1/ppermute | solution.py:33
  25.2 17.1 %collective-permute-start.4 = (bf16[2048,128]{1,0:T(8,128)(2,1)S(1)}, bf16[2048,128]{1,0:T(8,128)(2,1)S(1)}, u32[]{:S(2)}, u32[]{:S(2)}) collective-permute-start(bf16[2048,128]{1,0:T(8,128)(2,1)S(1)} %pad_maximum_fusion.2), channel_id=1, source_target_pairs={{0,4},{16,28},{4,8},{20,16},{8,12},{24,20},{12,0},{28,24},{1,5},{1... | collective-permute-start | bytes 1572872 | tf_op jit(solution)/shard_map/up0/ppermute | solution.py:33
  27.2 11.0 %collective-permute-start.10 = (bf16[1024,128]{1,0:T(8,128)(2,1)S(1)}, bf16[1024,128]{1,0:T(8,128)(2,1)S(1)}, u32[]{:S(2)}, u32[]{:S(2)}) collective-permute-start(bf16[1024,128]{1,0:T(8,128)(2,1)S(1)} %collective-permute-done.2.refs_2_), channel_id=1, source_target_pairs={{0,16},{16,0},{1,17},{17,1},{2,18},{18,2},{3,19},{19,3},{4,20},{20... | collective-permute-start | bytes 786440 | tf_op jit(solution)/shard_map/swap3/ppermute | solution.py:33
  28.0 9.1 %collective-permute-start.18 = (bf16[256,256]{1,0:T(8,128)(2,1)S(1)}, bf16[256,256]{1,0:T(8,128)(2,1)S(1)}, u32[]{:S(2)}, u32[]{:S(2)}) collective-permute-start(bf16[256,256]{1,0:T(8,128)(2,1)S(1)} %slice_add_fusion), channel_id=1, source_target_pairs={{0,32},{32,0},{1,33},{33,1},{2,34},{34,2},{3,35},{35,3},{4,36},{36... | collective-permute-start | bytes 393224 | tf_op jit(solution)/shard_map/zh/ppermute | solution.py:33
  37.2 8.6 %collective-permute-start.19 = (bf16[256,256]{1,0:T(8,128)(2,1)S(1)}, bf16[256,256]{1,0:T(8,128)(2,1)S(1)}, u32[]{:S(2)}, u32[]{:S(2)}) collective-permute-start(bf16[256,256]{1,0:T(8,128)(2,1)S(1)} %add.7), channel_id=1, source_target_pairs={{0,16},{16,0},{1,17},{17,1},{2,18},{18,2},{3,19},{19,3},{4,20},{20... | collective-permute-start | bytes 393224 | tf_op jit(solution)/shard_map/c2/ppermute | solution.py:33
  38.2 9.7 %collective-permute-start.11 = (bf16[2048,128]{1,0:T(8,128)(2,1)S(1)}, bf16[2048,128]{1,0:T(8,128)(2,1)S(1)}, u32[]{:S(2)}, u32[]{:S(2)}) collective-permute-start(bf16[2048,128]{1,0:T(8,128)(2,1)S(1)} %pad_maximum_fusion.3), channel_id=1, source_target_pairs={{0,4},{16,28},{4,8},{20,16},{8,12},{24,20},{12,0},{28,24},{1,5},{1... | collective-permute-start | bytes 1572872 | tf_op jit(solution)/shard_map/up3/ppermute | solution.py:33
  42.3 12.4 %collective-permute-start.8 = (bf16[1024,128]{1,0:T(8,128)(2,1)S(1)}, bf16[1024,128]{1,0:T(8,128)(2,1)S(1)}, u32[]{:S(2)}, u32[]{:S(2)}) collective-permute-start(bf16[1024,128]{1,0:T(8,128)(2,1)S(1)} %get-tuple-element.23), channel_id=1, source_target_pairs={{0,4},{16,28},{4,8},{20,16},{8,12},{24,20},{12,0},{28,24},{1,5},{1... | collective-permute-start | bytes 786440 | tf_op jit(solution)/shard_map/far0/ppermute | solution.py:33
  45.5 9.0 %collective-permute-start.21 = (bf16[256,256]{1,0:T(8,128)(2,1)S(1)}, bf16[256,256]{1,0:T(8,128)(2,1)S(1)}, u32[]{:S(2)}, u32[]{:S(2)}) collective-permute-start(bf16[256,256]{1,0:T(8,128)(2,1)S(1)} %add.7), channel_id=1, source_target_pairs={{0,128},{16,144},{64,192},{80,208},{128,0},{144,16},{192,64},{208,... | collective-permute-start | bytes 393224 | tf_op jit(solution)/shard_map/g2/ppermute | solution.py:33
  45.8 8.8 %collective-permute-start.20 = (bf16[512,256]{1,0:T(8,128)(2,1)S(1)}, bf16[512,256]{1,0:T(8,128)(2,1)S(1)}, u32[]{:S(2)}, u32[]{:S(2)}) collective-permute-start(bf16[512,256]{1,0:T(8,128)(2,1)S(1)} %pad_maximum_fusion.6.refs_11_), channel_id=1, source_target_pairs={{0,64},{16,208},{64,0},{80,144},{128,192},{144,80},{192,128},{208,... | collective-permute-start | bytes 786440 | tf_op jit(solution)/shard_map/g1/ppermute | solution.py:33
  47.5 14.8 %copy-start.1 = (s32[48]{0:T(128)S(1)}, s32[48]{0:T(128)}, u32[]{:S(2)}) copy-start(s32[48]{0:T(128)} %shard_map.46.table) | copy-start | bytes 580
  47.5 14.7 %collective-permute-start.7 = (bf16[3072,128]{1,0:T(8,128)(2,1)S(1)}, bf16[3072,128]{1,0:T(8,128)(2,1)S(1)}, u32[]{:S(2)}, u32[]{:S(2)}) collective-permute-start(bf16[3072,128]{1,0:T(8,128)(2,1)S(1)} %pad_maximum_fusion.1), channel_id=1, source_target_pairs={{0,16},{16,0},{1,17},{17,1},{2,18},{18,2},{3,19},{19,3},{4,20},{20... | collective-permute-start | bytes 2359304 | tf_op jit(solution)/shard_map/down/ppermute | solution.py:33
  48.0 14.3 %collective-permute-start.12 = (bf16[2048,128]{1,0:T(8,128)(2,1)S(1)}, bf16[2048,128]{1,0:T(8,128)(2,1)S(1)}, u32[]{:S(2)}, u32[]{:S(2)}) collective-permute-start(bf16[2048,128]{1,0:T(8,128)(2,1)S(1)} %pad_maximum_fusion.4), channel_id=1, source_target_pairs={{0,4},{16,28},{4,8},{20,16},{8,12},{24,20},{12,0},{28,24},{1,5},{1... | collective-permute-start | bytes 1572872 | tf_op jit(solution)/shard_map/far23/ppermute | solution.py:33
  54.6 7.7 %collective-permute-start.22 = (bf16[768,256]{1,0:T(8,128)(2,1)S(1)}, bf16[768,256]{1,0:T(8,128)(2,1)S(1)}, u32[]{:S(2)}, u32[]{:S(2)}) collective-permute-start(bf16[768,256]{1,0:T(8,128)(2,1)S(1)} %constant_dynamic-update-slice_fusion.2.refs_12_), channel_id=1, source_target_pairs={{0,16},{16,0},{1,17},{17,1},{2,18},{18,2},{3,19},{19,3},{4,20},{20... | collective-permute-start | bytes 1179656 | tf_op jit(solution)/shard_map/c34/ppermute | solution.py:33
  54.7 7.6 %collective-permute-start.9 = (bf16[1024,128]{1,0:T(8,128)(2,1)S(1)}, bf16[1024,128]{1,0:T(8,128)(2,1)S(1)}, u32[]{:S(2)}, u32[]{:S(2)}) collective-permute-start(bf16[1024,128]{1,0:T(8,128)(2,1)S(1)} %collective-permute-done.8.refs_5_), channel_id=1, source_target_pairs={{0,1},{16,17},{1,0},{17,16},{2,3},{18,19},{3,2},{19,18},{4,5},{20,... | collective-permute-start | bytes 786440 | tf_op jit(solution)/shard_map/far1/ppermute | solution.py:33
  55.0 7.3 %collective-permute-start.13 = (bf16[1024,128]{1,0:T(8,128)(2,1)S(1)}, bf16[1024,128]{1,0:T(8,128)(2,1)S(1)}, u32[]{:S(2)}, u32[]{:S(2)}) collective-permute-start(bf16[1024,128]{1,0:T(8,128)(2,1)S(1)} %get-tuple-element.21), channel_id=1, source_target_pairs={{0,16},{16,0},{1,17},{17,1},{2,18},{18,2},{3,19},{19,3},{4,20},{20... | collective-permute-start | bytes 786440 | tf_op jit(solution)/shard_map/down3/ppermute | solution.py:33

commit v5 on v4

--- a/solution.py
+++ b/solution.py
@@ -63,9 +63,11 @@
     y, z = (lax.axis_index(axis) for axis in VIR)
     one, two = (y + 3 + 2 * c) % NY, (y + 1 + 2 * c) % NY
     far = (y + 2) % NY
-    sources = [(y, z), (y, z ^ 1), (y, z ^ 2), (y, z ^ 3)]
-    for bit in range(NZ):
-        sources += [(one, z ^ bit), (two, z ^ bit), (far, z ^ bit)]
+    sources = [(y, z ^ bit) for bit in range(NZ)]
+    sources += [(one, z), (two, z), (two, z ^ 1), (two, z ^ 2), (far, z)]
+    sources += [(one, z ^ 1), (one, z ^ 2)]
+    sources += [(far, z ^ 1), (far, z ^ 2), (far, z ^ 3)]
+    sources += [(one, z ^ 3), (two, z ^ 3)]
     for i, (row, col) in enumerate(sources):
         inverse[row * NZ + col] = i
     for s in range(SYMS):
@@ -207,10 +209,9 @@
     both_swapped = swap("c34", both)
     parts = [pair, both, both_swapped]
     pieces = [(own, 0), (line, 0), (line, rows), (z3, 0)]
-    pieces += [(up0, 0), (down, 0), (far0, 0)]
-    pieces += [(up12, 0), (down, rows), (far1, 0)]
-    pieces += [(up12, rows), (down, 2 * rows), (far23, 0)]
-    pieces += [(up3, 0), (down3, 0), (far23, rows)]
+    pieces += [(up0, 0), (down, 0), (down, rows), (down, 2 * rows), (far0, 0)]
+    pieces += [(up12, 0), (up12, rows), (far1, 0), (far23, 0), (far23, rows)]
+    pieces += [(up3, 0), (down3, 0)]
     return table, pieces, parts
 
 
@@ -218,14 +219,21 @@
     count = len(refs) - 4
     pieces, parts = refs[: count - 3], refs[count - 3 : count]
     out, amps, slab, sems = refs[count:]
-    rows = amps.shape[1]
+    rows = amps.shape[0] // NK
 
     @pl.when(pl.program_id(0) == 0)
     def _():
         copies = []
-        for i, (which, start) in enumerate(spots):
-            source = pieces[which].at[pl.ds(start, rows)]
-            copies.append(pltpu.make_async_copy(source, amps.at[i], sems.at[i]))
+        i = 0
+        while i < NK:
+            which, start = spots[i]
+            run = 1
+            while i + run < NK and spots[i + run] == (which, start + run * rows):
+                run += 1
+            source = pieces[which].at[pl.ds(start, run * rows)]
+            target = amps.at[pl.ds(i * rows, run * rows)]
+            copies.append(pltpu.make_async_copy(source, target, sems.at[i]))
+            i += run
         place = 0
         for i, part in enumerate(parts):
             size = part.shape[0]
@@ -237,12 +245,13 @@
         for copy in copies:
             copy.wait()
 
-    block = pl.ds(pl.multiple_of(pl.program_id(0) * STEP, STEP), STEP)
+    shift = pl.program_id(0) * STEP
     depth = 2 * P_SIZE
     for l in range(NK):
-        pair = jnp.concatenate(
-            [amps[table[SLOTS + r * NK + l], block] for r in range(2)], axis=1
-        )
+        starts = [
+            pl.multiple_of(table[SLOTS + r * NK + l] * rows + shift, STEP) for r in range(2)
+        ]
+        pair = jnp.concatenate([amps[pl.ds(start, STEP)] for start in starts], axis=1)
         place = pl.multiple_of(table[HALVES + l // 2] * depth, depth)
         lane = (l % 2) * P_SIZE
         weights = slab[pl.ds(place, depth), lane : lane + P_SIZE]
@@ -269,7 +278,7 @@
             in_specs=[ANY] * (len(arrays) + len(parts)),
             out_specs=pl.BlockSpec((STEP, width), lambda i, table: (i, 0)),
             scratch_shapes=[
-                pltpu.VMEM((NK, rows, P_SIZE), jnp.bfloat16),
+                pltpu.VMEM((NK * rows, P_SIZE), jnp.bfloat16),
                 pltpu.VMEM((2 * NK * P_SIZE // 2, 2 * P_SIZE), jnp.bfloat16),
                 pltpu.SemaphoreType.DMA((NK + len(parts),)),
             ],

time: 68.9 us -> 68.8 us (level)
  no operation moved by 1% of the time
where the time goes in v5:
time: 68.8 us; the launch traced here: 68.6 us
  starting transfers between devices  34 us (49%)
  waiting for transfers between devices  21.7 us (32%)
  Pallas kernels  9.55 us (14%)
  other arithmetic  2.07 us (3%)
  local copies, waits for them, and re-layouts  0.91 us (1%)
    ppermute x23, starting transfers between devices, send(): return lax.ppermute(value, axes, pairs)  34 us
    ppermute x23, waiting for transfers between devices, send(): return lax.ppermute(value, axes, pairs)  21.7 us
    pallas_call x1, Pallas kernels, multiply(): pl.pallas_call(functools.partial(multiply_kernel, tuple(spots)), out_shap...  6.18 us
    pallas_call x1, Pallas kernels, cut(): pl.pallas_call(cut_kernel, out_shape=[shape] * NX, in_specs=[ANY], out_sp...  1.92 us
    pallas_call x1, Pallas kernels, make_table(): pl.pallas_call(table_kernel, out_shape=jax.ShapeDtypeStruct((TABLE,), jnp...  1.45 us
  transfers between devices with their start and end apart: 23, of which 8 were waited for; matrix products, arithmetic and copies ran while one was open for 4% of the time, Pallas kernels for 5%

profile of v5, /device:TPU:1, one launch (start us, length us, event | category | flops | bytes accessed | tf_op | source)
XLA Modules:
  0.0 68.6 jit_solution(15719863751540994321)
XLA Ops:
  0.0 3.2 %collective-permute-start.3 = (bf16[1024,128]{1,0:T(8,128)(2,1)}, bf16[1024,128]{1,0:T(8,128)(2,1)S(1)}, u32[]{:S(2)}, u32[]{:S(2)}) collective-permute-start(bf16[1024,128]{1,0:T(8,128)(2,1)} %refs_0_.1), channel_id=1, source_target_pairs={{0,16},{16,0},{1,17},{17,1},{2,18},{18,2},{3,19},{19,3},{4,20},{20... | collective-permute-start | bytes 786440 | tf_op jit(solution)/shard_map/swap0/ppermute | solution.py:33
  3.2 1.3 %collective-permute-start.1 = (bf16[1024,128]{1,0:T(8,128)(2,1)}, bf16[1024,128]{1,0:T(8,128)(2,1)S(1)}, u32[]{:S(2)}, u32[]{:S(2)}) collective-permute-start(bf16[1024,128]{1,0:T(8,128)(2,1)} %refs_0_.1), channel_id=1, source_target_pairs={{0,2},{16,18},{1,3},{17,19},{2,0},{18,16},{3,1},{19,17},{4,6},{20,... | collective-permute-start | bytes 786440 | tf_op jit(solution)/shard_map/z2/ppermute | solution.py:33
  4.5 1.6 %collective-permute-start = (bf16[1024,128]{1,0:T(8,128)(2,1)}, bf16[1024,128]{1,0:T(8,128)(2,1)S(1)}, u32[]{:S(2)}, u32[]{:S(2)}) collective-permute-start(bf16[1024,128]{1,0:T(8,128)(2,1)} %refs_0_.1), channel_id=1, source_target_pairs={{0,1},{16,17},{1,0},{17,16},{2,3},{18,19},{3,2},{19,18},{4,5},{20,... | collective-permute-start | bytes 786440 | tf_op jit(solution)/shard_map/z1/ppermute | solution.py:33
  6.1 1.9 %shard_map.47 = (bf16[128,512]{1,0:T(8,128)(2,1)}, bf16[128,512]{1,0:T(8,128)(2,1)}, bf16[128,512]{1,0:T(8,128)(2,1)}, bf16[128,512]{1,0:T(8,128)(2,1)}) custom-call(bf16[128,2048]{1,0:T(8,128)(2,1)} %integrals.1), custom_call_target="tpu_custom_call" | custom-call | tf_op jit(solution)/shard_map/pallas_call | solution.py:149
  8.1 2.8 %collective-permute-start.14 = (bf16[128,512]{1,0:T(8,128)(2,1)}, bf16[128,512]{1,0:T(8,128)(2,1)S(1)}, u32[]{:S(2)}, u32[]{:S(2)}) collective-permute-start(bf16[128,512]{1,0:T(8,128)(2,1)} %get-tuple-element.15), channel_id=1, source_target_pairs={{0,128},{16,144},{64,192},{80,208},{128,0},{144,16},{192,64},{208,... | collective-permute-start | bytes 393224 | tf_op jit(solution)/shard_map/r2/ppermute | solution.py:33
  10.9 0.8 %collective-permute-start.15 = (bf16[128,512]{1,0:T(8,128)(2,1)}, bf16[128,512]{1,0:T(8,128)(2,1)S(1)}, u32[]{:S(2)}, u32[]{:S(2)}) collective-permute-start(bf16[128,512]{1,0:T(8,128)(2,1)} %get-tuple-element.17), channel_id=1, source_target_pairs={{0,16},{16,0},{1,17},{17,1},{2,18},{18,2},{3,19},{19,3},{4,20},{20... | collective-permute-start | bytes 393224 | tf_op jit(solution)/shard_map/r0/ppermute | solution.py:33
  11.7 1.5 %shard_map.46.table = s32[48]{0:T(128)} custom-call(s32[16]{0:T(128)} %contract.1, s32[16]{0:T(128)} %column.1), custom_call_target="tpu_custom_call" | custom-call | tf_op jit(solution)/shard_map/pallas_call | solution.py:114
  13.2 0.7 %broadcast_compare_fusion.3 = (pred[8]{0:T(512)(128)(4,1)S(1)}, pred[8]{0:T(512)(128)(4,1)S(1)}, pred[8]{0:T(512)(128)(4,1)S(1)}, pred[8]{0:T(512)(128)(4,1)S(1)}) fusion(s32[48]{0:T(128)} %shard_map.46.table), kind=kLoop, calls=%fused_computation.24 | loop fusion | flops 32 | bytes 64 | tf_op jit(solution)/shard_map/eq | solution.py:163
  13.9 0.1 eq.74
  14.0 0.1 eq.82
  14.1 0.1 broadcast_bitcast_fusion.1
  14.2 0.1 eq.86
  14.3 0.1 broadcast_bitcast_fusion
  14.4 0.1 broadcast_bitcast_fusion.3
  14.4 0.1 eq.78
  14.5 1.0 %pad_maximum_fusion.5 = bf16[256,512]{1,0:T(8,128)(2,1)S(1)} fusion(bf16[128,512]{1,0:T(8,128)(2,1)S(1)} %collective-permute-done.15, bf16[128,512]{1,0:T(8,128)(2,1)} %get-tuple-element.16), kind=kLoop, calls=%fused_computation.5 | loop fusion | flops 524288 | bytes 524288 | tf_op jit(solution)/shard_map/concatenate | solution.py:179
  15.5 0.9 %collective-permute-start.16 = (bf16[256,512]{1,0:T(8,128)(2,1)S(1)}, bf16[256,512]{1,0:T(8,128)(2,1)S(1)}, u32[]{:S(2)}, u32[]{:S(2)}) collective-permute-start(bf16[256,512]{1,0:T(8,128)(2,1)S(1)} %pad_maximum_fusion.5), channel_id=1, source_target_pairs={{0,64},{16,208},{64,0},{80,144},{128,192},{144,80},{192,128},{208,... | collective-permute-start | bytes 786440 | tf_op jit(solution)/shard_map/r1/ppermute | solution.py:33
  16.5 0.0 copy-start
  16.5 1.5 %collective-permute-done.1 = bf16[1024,128]{1,0:T(8,128)(2,1)S(1)} collective-permute-done((bf16[1024,128]{1,0:T(8,128)(2,1)}, bf16[1024,128]{1,0:T(8,128)(2,1)S(1)}, u32[]{:S(2)}, u32[]{:S(2)}) %collective-permute-start.1) | collective-permute-done | bytes 262176 | tf_op jit(solution)/shard_map/z2/ppermute | solution.py:33
  18.0 1.0 %collective-permute-start.5 = (bf16[2048,128]{1,0:T(8,128)(2,1)S(1)}, bf16[2048,128]{1,0:T(8,128)(2,1)S(1)}, u32[]{:S(2)}, u32[]{:S(2)}) collective-permute-start(bf16[2048,128]{1,0:T(8,128)(2,1)S(1)} %constant_dynamic-update-slice_fusion.refs_1_), channel_id=1, source_target_pairs={{0,16},{16,0},{1,17},{17,1},{2,18},{18,2},{3,19},{19,3},{4,20},{20... | collective-permute-start | bytes 1572872 | tf_op jit(solution)/shard_map/turned/ppermute | solution.py:33
  19.1 0.1 broadcast_bitcast_fusion.2
  19.2 0.3 collective-permute-start.2
  19.4 2.6 %collective-permute-done.16 = bf16[256,512]{1,0:T(8,128)(2,1)S(1)} collective-permute-done((bf16[256,512]{1,0:T(8,128)(2,1)S(1)}, bf16[256,512]{1,0:T(8,128)(2,1)S(1)}, u32[]{:S(2)}, u32[]{:S(2)}) %collective-permute-start.16) | collective-permute-done | bytes 262176 | tf_op jit(solution)/shard_map/r1/ppermute | solution.py:33
  22.0 0.1 pad_maximum_fusion
  22.1 2.8 %collective-permute-start.6 = (bf16[4096,128]{1,0:T(8,128)(2,1)S(1)}, bf16[4096,128]{1,0:T(8,128)(2,1)S(1)}, u32[]{:S(2)}, u32[]{:S(2)}) collective-permute-start(bf16[4096,128]{1,0:T(8,128)(2,1)S(1)} %pad_maximum_fusion), channel_id=1, source_target_pairs={{0,4},{16,28},{4,8},{20,16},{8,12},{24,20},{12,0},{28,24},{1,5},{1... | collective-permute-start | bytes 3145736 | tf_op jit(solution)/shard_map/up12/ppermute | solution.py:33
  24.9 0.1 select_select_fusion
  25.0 0.1 collective-permute-start.17
  25.2 0.5 collective-permute-start.4
  25.7 1.4 %collective-permute-done.2.refs_2_ = bf16[1024,128]{1,0:T(8,128)(2,1)S(1)} collective-permute-done((bf16[1024,128]{1,0:T(8,128)(2,1)S(1)}, bf16[1024,128]{1,0:T(8,128)(2,1)S(1)}, u32[]{:S(2)}, u32[]{:S(2)}) %collective-permute-start.2) | collective-permute-done | bytes 262176 | tf_op jit(solution)/shard_map/z3/ppermute | solution.py:33
  27.2 0.8 %collective-permute-start.10 = (bf16[1024,128]{1,0:T(8,128)(2,1)S(1)}, bf16[1024,128]{1,0:T(8,128)(2,1)S(1)}, u32[]{:S(2)}, u32[]{:S(2)}) collective-permute-start(bf16[1024,128]{1,0:T(8,128)(2,1)S(1)} %collective-permute-done.2.refs_2_), channel_id=1, source_target_pairs={{0,16},{16,0},{1,17},{17,1},{2,18},{18,2},{3,19},{19,3},{4,20},{20... | collective-permute-start | bytes 786440 | tf_op jit(solution)/shard_map/swap3/ppermute | solution.py:33
  28.0 5.0 %collective-permute-start.18 = (bf16[256,256]{1,0:T(8,128)(2,1)S(1)}, bf16[256,256]{1,0:T(8,128)(2,1)S(1)}, u32[]{:S(2)}, u32[]{:S(2)}) collective-permute-start(bf16[256,256]{1,0:T(8,128)(2,1)S(1)} %slice_add_fusion), channel_id=1, source_target_pairs={{0,32},{32,0},{1,33},{33,1},{2,34},{34,2},{3,35},{35,3},{4,36},{36... | collective-permute-start | bytes 393224 | tf_op jit(solution)/shard_map/zh/ppermute | solution.py:33
  33.0 4.1 %collective-permute-done.18 = bf16[256,256]{1,0:T(8,128)(2,1)S(1)} collective-permute-done((bf16[256,256]{1,0:T(8,128)(2,1)S(1)}, bf16[256,256]{1,0:T(8,128)(2,1)S(1)}, u32[]{:S(2)}, u32[]{:S(2)}) %collective-permute-start.18) | collective-permute-done | bytes 131104 | tf_op jit(solution)/shard_map/zh/ppermute | solution.py:33
  37.2 1.0 %collective-permute-start.19 = (bf16[256,256]{1,0:T(8,128)(2,1)S(1)}, bf16[256,256]{1,0:T(8,128)(2,1)S(1)}, u32[]{:S(2)}, u32[]{:S(2)}) collective-permute-start(bf16[256,256]{1,0:T(8,128)(2,1)S(1)} %add.7), channel_id=1, source_target_pairs={{0,16},{16,0},{1,17},{17,1},{2,18},{18,2},{3,19},{19,3},{4,20},{20... | collective-permute-start | bytes 393224 | tf_op jit(solution)/shard_map/c2/ppermute | solution.py:33
  38.2 2.4 %collective-permute-start.11 = (bf16[2048,128]{1,0:T(8,128)(2,1)S(1)}, bf16[2048,128]{1,0:T(8,128)(2,1)S(1)}, u32[]{:S(2)}, u32[]{:S(2)}) collective-permute-start(bf16[2048,128]{1,0:T(8,128)(2,1)S(1)} %pad_maximum_fusion.3), channel_id=1, source_target_pairs={{0,4},{16,28},{4,8},{20,16},{8,12},{24,20},{12,0},{28,24},{1,5},{1... | collective-permute-start | bytes 1572872 | tf_op jit(solution)/shard_map/up3/ppermute | solution.py:33
  40.5 1.8 %collective-permute-done.4.refs_3_ = bf16[2048,128]{1,0:T(8,128)(2,1)S(1)} collective-permute-done((bf16[2048,128]{1,0:T(8,128)(2,1)S(1)}, bf16[2048,128]{1,0:T(8,128)(2,1)S(1)}, u32[]{:S(2)}, u32[]{:S(2)}) %collective-permute-start.4) | collective-permute-done | bytes 524320 | tf_op jit(solution)/shard_map/up0/ppermute | solution.py:33
  42.3 3.2 %collective-permute-start.8 = (bf16[1024,128]{1,0:T(8,128)(2,1)S(1)}, bf16[1024,128]{1,0:T(8,128)(2,1)S(1)}, u32[]{:S(2)}, u32[]{:S(2)}) collective-permute-start(bf16[1024,128]{1,0:T(8,128)(2,1)S(1)} %get-tuple-element.23), channel_id=1, source_target_pairs={{0,4},{16,28},{4,8},{20,16},{8,12},{24,20},{12,0},{28,24},{1,5},{1... | collective-permute-start | bytes 786440 | tf_op jit(solution)/shard_map/far0/ppermute | solution.py:33
  45.5 0.2 collective-permute-start.21
  45.8 1.7 %collective-permute-start.20 = (bf16[512,256]{1,0:T(8,128)(2,1)S(1)}, bf16[512,256]{1,0:T(8,128)(2,1)S(1)}, u32[]{:S(2)}, u32[]{:S(2)}) collective-permute-start(bf16[512,256]{1,0:T(8,128)(2,1)S(1)} %pad_maximum_fusion.6.refs_11_), channel_id=1, source_target_pairs={{0,64},{16,208},{64,0},{80,144},{128,192},{144,80},{192,128},{208,... | collective-permute-start | bytes 786440 | tf_op jit(solution)/shard_map/g1/ppermute | solution.py:33
  47.5 0.1 pad_maximum_fusion.1
  47.5 0.3 collective-permute-start.7
  47.8 0.1 collective-permute-done.11.refs_9_
  48.0 3.2 %collective-permute-start.12 = (bf16[2048,128]{1,0:T(8,128)(2,1)S(1)}, bf16[2048,128]{1,0:T(8,128)(2,1)S(1)}, u32[]{:S(2)}, u32[]{:S(2)}) collective-permute-start(bf16[2048,128]{1,0:T(8,128)(2,1)S(1)} %pad_maximum_fusion.4), channel_id=1, source_target_pairs={{0,4},{16,28},{4,8},{20,16},{8,12},{24,20},{12,0},{28,24},{1,5},{1... | collective-permute-start | bytes 1572872 | tf_op jit(solution)/shard_map/far23/ppermute | solution.py:33
  51.2 3.4 %collective-permute-done.20 = bf16[512,256]{1,0:T(8,128)(2,1)S(1)} collective-permute-done((bf16[512,256]{1,0:T(8,128)(2,1)S(1)}, bf16[512,256]{1,0:T(8,128)(2,1)S(1)}, u32[]{:S(2)}, u32[]{:S(2)}) %collective-permute-start.20) | collective-permute-done | bytes 262176 | tf_op jit(solution)/shard_map/g1/ppermute | solution.py:33
  54.6 0.1 collective-permute-start.22
  54.7 0.3 collective-permute-start.9
  55.0 0.4 collective-permute-start.13
  55.4 6.8 %collective-permute-done.9.refs_7_ = bf16[1024,128]{1,0:T(8,128)(2,1)S(1)} collective-permute-done((bf16[1024,128]{1,0:T(8,128)(2,1)S(1)}, bf16[1024,128]{1,0:T(8,128)(2,1)S(1)}, u32[]{:S(2)}, u32[]{:S(2)}) %collective-permute-start.9) | collective-permute-done | bytes 262176 | tf_op jit(solution)/shard_map/far1/ppermute | solution.py:33
  62.3 6.2 %shard_map.48 = f32[1024,2048]{1,0:T(8,128)} custom-call(s32[48]{0:T(128)S(1)} %copy-done.1, bf16[1024,128]{1,0:T(8,128)(2,1)S(1)} %copy-done, bf16[2048,128]{1,0:T(8,128)(2,1)S(1)} %constant_dynamic-update-slice_fusion.refs_1_, bf16[1024,128]{1,0:T(8,128)(2,1)S(1)} %collective-permute-done.2.refs_2_, bf16[2048,128]{1,0:T(8,128)(2,1)S(1)} %collective-permute-done.4.refs_3_, ...), custom_call_target="tpu_custom_call" | custom-call | flops 1073741824 | bytes 8388608 | tf_op jit(solution)/shard_map/pallas_call | solution.py:272
  (38 shorter events, 0.5 us)
Async XLA Ops:
  0.0 25.1 %collective-permute-start.3 = (bf16[1024,128]{1,0:T(8,128)(2,1)}, bf16[1024,128]{1,0:T(8,128)(2,1)S(1)}, u32[]{:S(2)}, u32[]{:S(2)}) collective-permute-start(bf16[1024,128]{1,0:T(8,128)(2,1)} %refs_0_.1), channel_id=1, source_target_pairs={{0,16},{16,0},{1,17},{17,1},{2,18},{18,2},{3,19},{19,3},{4,20},{20... | collective-permute-start | bytes 786440 | tf_op jit(solution)/shard_map/swap0/ppermute | solution.py:33
  3.2 14.8 %collective-permute-start.1 = (bf16[1024,128]{1,0:T(8,128)(2,1)}, bf16[1024,128]{1,0:T(8,128)(2,1)S(1)}, u32[]{:S(2)}, u32[]{:S(2)}) collective-permute-start(bf16[1024,128]{1,0:T(8,128)(2,1)} %refs_0_.1), channel_id=1, source_target_pairs={{0,2},{16,18},{1,3},{17,19},{2,0},{18,16},{3,1},{19,17},{4,6},{20,... | collective-permute-start | bytes 786440 | tf_op jit(solution)/shard_map/z2/ppermute | solution.py:33
  4.5 11.9 %collective-permute-start = (bf16[1024,128]{1,0:T(8,128)(2,1)}, bf16[1024,128]{1,0:T(8,128)(2,1)S(1)}, u32[]{:S(2)}, u32[]{:S(2)}) collective-permute-start(bf16[1024,128]{1,0:T(8,128)(2,1)} %refs_0_.1), channel_id=1, source_target_pairs={{0,1},{16,17},{1,0},{17,16},{2,3},{18,19},{3,2},{19,18},{4,5},{20,... | collective-permute-start | bytes 786440 | tf_op jit(solution)/shard_map/z1/ppermute | solution.py:33
  8.1 16.9 %collective-permute-start.14 = (bf16[128,512]{1,0:T(8,128)(2,1)}, bf16[128,512]{1,0:T(8,128)(2,1)S(1)}, u32[]{:S(2)}, u32[]{:S(2)}) collective-permute-start(bf16[128,512]{1,0:T(8,128)(2,1)} %get-tuple-element.15), channel_id=1, source_target_pairs={{0,128},{16,144},{64,192},{80,208},{128,0},{144,16},{192,64},{208,... | collective-permute-start | bytes 393224 | tf_op jit(solution)/shard_map/r2/ppermute | solution.py:33
  10.9 3.6 %collective-permute-start.15 = (bf16[128,512]{1,0:T(8,128)(2,1)}, bf16[128,512]{1,0:T(8,128)(2,1)S(1)}, u32[]{:S(2)}, u32[]{:S(2)}) collective-permute-start(bf16[128,512]{1,0:T(8,128)(2,1)} %get-tuple-element.17), channel_id=1, source_target_pairs={{0,16},{16,0},{1,17},{17,1},{2,18},{18,2},{3,19},{19,3},{4,20},{20... | collective-permute-start | bytes 393224 | tf_op jit(solution)/shard_map/r0/ppermute | solution.py:33
  14.5 10.4 %copy-start.2 = (bf16[128,512]{1,0:T(8,128)(2,1)S(1)}, bf16[128,512]{1,0:T(8,128)(2,1)}, u32[]{:S(2)}) copy-start(bf16[128,512]{1,0:T(8,128)(2,1)} %get-tuple-element.18) | copy-start | bytes 393220
  15.5 6.5 %collective-permute-start.16 = (bf16[256,512]{1,0:T(8,128)(2,1)S(1)}, bf16[256,512]{1,0:T(8,128)(2,1)S(1)}, u32[]{:S(2)}, u32[]{:S(2)}) collective-permute-start(bf16[256,512]{1,0:T(8,128)(2,1)S(1)} %pad_maximum_fusion.5), channel_id=1, source_target_pairs={{0,64},{16,208},{64,0},{80,144},{128,192},{144,80},{192,128},{208,... | collective-permute-start | bytes 786440 | tf_op jit(solution)/shard_map/r1/ppermute | solution.py:33
  16.5 8.7 %copy-start = (bf16[1024,128]{1,0:T(8,128)(2,1)S(1)}, bf16[1024,128]{1,0:T(8,128)(2,1)}, u32[]{:S(2)}) copy-start(bf16[1024,128]{1,0:T(8,128)(2,1)} %refs_0_.1) | copy-start | bytes 786436
  18.0 4.0 %collective-permute-start.5 = (bf16[2048,128]{1,0:T(8,128)(2,1)S(1)}, bf16[2048,128]{1,0:T(8,128)(2,1)S(1)}, u32[]{:S(2)}, u32[]{:S(2)}) collective-permute-start(bf16[2048,128]{1,0:T(8,128)(2,1)S(1)} %constant_dynamic-update-slice_fusion.refs_1_), channel_id=1, source_target_pairs={{0,16},{16,0},{1,17},{17,1},{2,18},{18,2},{3,19},{19,3},{4,20},{20... | collective-permute-start | bytes 1572872 | tf_op jit(solution)/shard_map/turned/ppermute | solution.py:33
  19.2 8.0 %collective-permute-start.2 = (bf16[1024,128]{1,0:T(8,128)(2,1)S(1)}, bf16[1024,128]{1,0:T(8,128)(2,1)S(1)}, u32[]{:S(2)}, u32[]{:S(2)}) collective-permute-start(bf16[1024,128]{1,0:T(8,128)(2,1)S(1)} %collective-permute-done.1), channel_id=1, source_target_pairs={{0,1},{16,17},{1,0},{17,16},{2,3},{18,19},{3,2},{19,18},{4,5},{20,... | collective-permute-start | bytes 786440 | tf_op jit(solution)/shard_map/z3/ppermute | solution.py:33
  22.1 16.1 %collective-permute-start.6 = (bf16[4096,128]{1,0:T(8,128)(2,1)S(1)}, bf16[4096,128]{1,0:T(8,128)(2,1)S(1)}, u32[]{:S(2)}, u32[]{:S(2)}) collective-permute-start(bf16[4096,128]{1,0:T(8,128)(2,1)S(1)} %pad_maximum_fusion), channel_id=1, source_target_pairs={{0,4},{16,28},{4,8},{20,16},{8,12},{24,20},{12,0},{28,24},{1,5},{1... | collective-permute-start | bytes 3145736 | tf_op jit(solution)/shard_map/up12/ppermute | solution.py:33
  25.0 2.9 %collective-permute-start.17 = (bf16[256,256]{1,0:T(8,128)(2,1)S(1)}, bf16[256,256]{1,0:T(8,128)(2,1)S(1)}, u32[]{:S(2)}, u32[]{:S(2)}) collective-permute-start(bf16[256,256]{1,0:T(8,128)(2,1)S(1)} %slice.61), channel_id=1, source_target_pairs={{0,16},{16,0},{1,17},{17,1},{2,18},{18,2},{3,19},{19,3},{4,20},{20... | collective-permute-start | bytes 393224 | tf_op jit(solution)/shard_map/c1/ppermute | solution.py:33
  25.2 17.1 %collective-permute-start.4 = (bf16[2048,128]{1,0:T(8,128)(2,1)S(1)}, bf16[2048,128]{1,0:T(8,128)(2,1)S(1)}, u32[]{:S(2)}, u32[]{:S(2)}) collective-permute-start(bf16[2048,128]{1,0:T(8,128)(2,1)S(1)} %pad_maximum_fusion.2), channel_id=1, source_target_pairs={{0,4},{16,28},{4,8},{20,16},{8,12},{24,20},{12,0},{28,24},{1,5},{1... | collective-permute-start | bytes 1572872 | tf_op jit(solution)/shard_map/up0/ppermute | solution.py:33
  27.2 11.0 %collective-permute-start.10 = (bf16[1024,128]{1,0:T(8,128)(2,1)S(1)}, bf16[1024,128]{1,0:T(8,128)(2,1)S(1)}, u32[]{:S(2)}, u32[]{:S(2)}) collective-permute-start(bf16[1024,128]{1,0:T(8,128)(2,1)S(1)} %collective-permute-done.2.refs_2_), channel_id=1, source_target_pairs={{0,16},{16,0},{1,17},{17,1},{2,18},{18,2},{3,19},{19,3},{4,20},{20... | collective-permute-start | bytes 786440 | tf_op jit(solution)/shard_map/swap3/ppermute | solution.py:33
  28.0 9.1 %collective-permute-start.18 = (bf16[256,256]{1,0:T(8,128)(2,1)S(1)}, bf16[256,256]{1,0:T(8,128)(2,1)S(1)}, u32[]{:S(2)}, u32[]{:S(2)}) collective-permute-start(bf16[256,256]{1,0:T(8,128)(2,1)S(1)} %slice_add_fusion), channel_id=1, source_target_pairs={{0,32},{32,0},{1,33},{33,1},{2,34},{34,2},{3,35},{35,3},{4,36},{36... | collective-permute-start | bytes 393224 | tf_op jit(solution)/shard_map/zh/ppermute | solution.py:33
  37.2 8.6 %collective-permute-start.19 = (bf16[256,256]{1,0:T(8,128)(2,1)S(1)}, bf16[256,256]{1,0:T(8,128)(2,1)S(1)}, u32[]{:S(2)}, u32[]{:S(2)}) collective-permute-start(bf16[256,256]{1,0:T(8,128)(2,1)S(1)} %add.7), channel_id=1, source_target_pairs={{0,16},{16,0},{1,17},{17,1},{2,18},{18,2},{3,19},{19,3},{4,20},{20... | collective-permute-start | bytes 393224 | tf_op jit(solution)/shard_map/c2/ppermute | solution.py:33
  38.2 9.7 %collective-permute-start.11 = (bf16[2048,128]{1,0:T(8,128)(2,1)S(1)}, bf16[2048,128]{1,0:T(8,128)(2,1)S(1)}, u32[]{:S(2)}, u32[]{:S(2)}) collective-permute-start(bf16[2048,128]{1,0:T(8,128)(2,1)S(1)} %pad_maximum_fusion.3), channel_id=1, source_target_pairs={{0,4},{16,28},{4,8},{20,16},{8,12},{24,20},{12,0},{28,24},{1,5},{1... | collective-permute-start | bytes 1572872 | tf_op jit(solution)/shard_map/up3/ppermute | solution.py:33
  42.3 12.4 %collective-permute-start.8 = (bf16[1024,128]{1,0:T(8,128)(2,1)S(1)}, bf16[1024,128]{1,0:T(8,128)(2,1)S(1)}, u32[]{:S(2)}, u32[]{:S(2)}) collective-permute-start(bf16[1024,128]{1,0:T(8,128)(2,1)S(1)} %get-tuple-element.23), channel_id=1, source_target_pairs={{0,4},{16,28},{4,8},{20,16},{8,12},{24,20},{12,0},{28,24},{1,5},{1... | collective-permute-start | bytes 786440 | tf_op jit(solution)/shard_map/far0/ppermute | solution.py:33
  45.5 9.0 %collective-permute-start.21 = (bf16[256,256]{1,0:T(8,128)(2,1)S(1)}, bf16[256,256]{1,0:T(8,128)(2,1)S(1)}, u32[]{:S(2)}, u32[]{:S(2)}) collective-permute-start(bf16[256,256]{1,0:T(8,128)(2,1)S(1)} %add.7), channel_id=1, source_target_pairs={{0,128},{16,144},{64,192},{80,208},{128,0},{144,16},{192,64},{208,... | collective-permute-start | bytes 393224 | tf_op jit(solution)/shard_map/g2/ppermute | solution.py:33
  45.8 8.8 %collective-permute-start.20 = (bf16[512,256]{1,0:T(8,128)(2,1)S(1)}, bf16[512,256]{1,0:T(8,128)(2,1)S(1)}, u32[]{:S(2)}, u32[]{:S(2)}) collective-permute-start(bf16[512,256]{1,0:T(8,128)(2,1)S(1)} %pad_maximum_fusion.6.refs_11_), channel_id=1, source_target_pairs={{0,64},{16,208},{64,0},{80,144},{128,192},{144,80},{192,128},{208,... | collective-permute-start | bytes 786440 | tf_op jit(solution)/shard_map/g1/ppermute | solution.py:33
  47.5 14.8 %copy-start.1 = (s32[48]{0:T(128)S(1)}, s32[48]{0:T(128)}, u32[]{:S(2)}) copy-start(s32[48]{0:T(128)} %shard_map.46.table) | copy-start | bytes 580
  47.5 14.7 %collective-permute-start.7 = (bf16[3072,128]{1,0:T(8,128)(2,1)S(1)}, bf16[3072,128]{1,0:T(8,128)(2,1)S(1)}, u32[]{:S(2)}, u32[]{:S(2)}) collective-permute-start(bf16[3072,128]{1,0:T(8,128)(2,1)S(1)} %pad_maximum_fusion.1), channel_id=1, source_target_pairs={{0,16},{16,0},{1,17},{17,1},{2,18},{18,2},{3,19},{19,3},{4,20},{20... | collective-permute-start | bytes 2359304 | tf_op jit(solution)/shard_map/down/ppermute | solution.py:33
  48.0 14.3 %collective-permute-start.12 = (bf16[2048,128]{1,0:T(8,128)(2,1)S(1)}, bf16[2048,128]{1,0:T(8,128)(2,1)S(1)}, u32[]{:S(2)}, u32[]{:S(2)}) collective-permute-start(bf16[2048,128]{1,0:T(8,128)(2,1)S(1)} %pad_maximum_fusion.4), channel_id=1, source_target_pairs={{0,4},{16,28},{4,8},{20,16},{8,12},{24,20},{12,0},{28,24},{1,5},{1... | collective-permute-start | bytes 1572872 | tf_op jit(solution)/shard_map/far23/ppermute | solution.py:33
  54.6 7.7 %collective-permute-start.22 = (bf16[768,256]{1,0:T(8,128)(2,1)S(1)}, bf16[768,256]{1,0:T(8,128)(2,1)S(1)}, u32[]{:S(2)}, u32[]{:S(2)}) collective-permute-start(bf16[768,256]{1,0:T(8,128)(2,1)S(1)} %constant_dynamic-update-slice_fusion.2.refs_12_), channel_id=1, source_target_pairs={{0,16},{16,0},{1,17},{17,1},{2,18},{18,2},{3,19},{19,3},{4,20},{20... | collective-permute-start | bytes 1179656 | tf_op jit(solution)/shard_map/c34/ppermute | solution.py:33
  54.7 7.6 %collective-permute-start.9 = (bf16[1024,128]{1,0:T(8,128)(2,1)S(1)}, bf16[1024,128]{1,0:T(8,128)(2,1)S(1)}, u32[]{:S(2)}, u32[]{:S(2)}) collective-permute-start(bf16[1024,128]{1,0:T(8,128)(2,1)S(1)} %collective-permute-done.8.refs_5_), channel_id=1, source_target_pairs={{0,1},{16,17},{1,0},{17,16},{2,3},{18,19},{3,2},{19,18},{4,5},{20,... | collective-permute-start | bytes 786440 | tf_op jit(solution)/shard_map/far1/ppermute | solution.py:33
  55.0 7.3 %collective-permute-start.13 = (bf16[1024,128]{1,0:T(8,128)(2,1)S(1)}, bf16[1024,128]{1,0:T(8,128)(2,1)S(1)}, u32[]{:S(2)}, u32[]{:S(2)}) collective-permute-start(bf16[1024,128]{1,0:T(8,128)(2,1)S(1)} %get-tuple-element.21), channel_id=1, source_target_pairs={{0,16},{16,0},{1,17},{17,1},{2,18},{18,2},{3,19},{19,3},{4,20},{20... | collective-permute-start | bytes 786440 | tf_op jit(solution)/shard_map/down3/ppermute | solution.py:33
